TPU v7x, 512 devices: a whole 4x4x16 slice. The times are simulated.
512 devices in a mesh: seq: 64 (over z, y_lo, core), head: 8 (over x, y_hi).
Axes of the slice: x: 4, y: 4 (y_hi: 2, y_lo: 2; y = y_hi * 2 + y_lo), z: 16, core: 2. Of those that a mesh axis runs over, the one named last changes fastest.
Arguments:
- queries: bfloat16 [32768, 4096], P(('seq', 'head')), may hold values from -64 to 64
- keys: bfloat16 [32768, 1024], P(('seq', 'head')), may hold values from -6 to 6
- values: bfloat16 [32768, 1024], P(('seq', 'head')), may hold values from -6 to 6
- level_bias: float32 [32, 6], P('head'), may hold values from -1 to 2
- anchor_bias: float32 [32], P('head'), may hold values from 1 to 4
- partners: int32 [64, 6], P('seq'), may hold values from 0 to 63, as said below
- anchor_positions: int32 [64], replicated, may hold values from 0 to 32767, as said below
Outputs:
- attended: bfloat16 [32768, 4096], P(('seq', 'head'))
Inputs may be any that keep to these rules, and one draw needn't show every extreme that they name: `partners`: row b holds b XOR 2**j once for each j of 0 to 5, in an order drawn for each block. `anchor_positions`: distinct positions.
All inputs are finite; a program needn't handle non-finite values.
Results may differ from a plain program's by a relative error of at most 0.0045.
Values may be sent and summed in bfloat16 or wider, within the bound.
No kernel may reach another device: no remote copies, remote signals or barrier semaphores. Data moves between devices by JAX's collectives and lax.ppermute only.
A program may use at most 128 MiB of HBM per device.

v0:
```python
import jax
import jax.numpy as jnp
from jax import lax
from jax.sharding import PartitionSpec as P

HD = 128


def partner_2(value, axis, stride):
    return lax.ppermute(value, axis, [(i, i ^ 1 << stride) for i in range(lax.axis_size(axis))])


def absorb(softmax_state, query_heads, key_block, value_block, score_bias, score_scale):
    running_max, running_sum, weighted = softmax_state
    kv_local = query_heads.shape[1]
    head_dim = query_heads.shape[3]
    key_heads = key_block.reshape(key_block.shape[0], kv_local, head_dim)
    value_heads = value_block.reshape(value_block.shape[0], kv_local, head_dim)
    scores = jnp.einsum(
        "tkgd,skd->kgts", query_heads, key_heads, preferred_element_type=jnp.float32
    )
    scores = scores * score_scale + score_bias[:, :, None, None]
    new_max = jnp.maximum(running_max, jnp.max(scores, axis=-1))
    rescale = jnp.exp(running_max - new_max)
    weights = jnp.exp(scores - new_max[..., None])
    running_sum = running_sum * rescale + jnp.sum(weights, axis=-1)
    update = jnp.einsum(
        "kgts,skd->kgtd",
        weights.astype(jnp.bfloat16),
        value_heads,
        preferred_element_type=jnp.float32,
    )
    weighted = weighted * rescale[..., None] + update
    return (new_max, running_sum, weighted)


def on_device(queries, keys, values, level_bias, anchor_bias, partners, anchor_positions):
    query_rows, key_rows, value_rows = (
        lax.all_to_all(queries, "head", split_axis=1, concat_axis=0, tiled=True),
        lax.all_to_all(keys, "head", split_axis=1, concat_axis=0, tiled=True),
        lax.all_to_all(values, "head", split_axis=1, concat_axis=0, tiled=True),
    )
    block_rows = query_rows.shape[0]
    head_dim = HD
    kv_local = key_rows.shape[1] // head_dim
    group_size = level_bias.shape[0] // kv_local
    score_scale = head_dim ** (-0.5)
    query_heads = query_rows.reshape(block_rows, kv_local, group_size, head_dim)
    block_index = lax.axis_index("seq")
    level_count = lax.axis_size("seq").bit_length() - 1
    token_index = block_index * block_rows + jnp.arange(block_rows, dtype=jnp.int32)
    selector = (anchor_positions[:, None] == token_index[None, :]).astype(jnp.bfloat16)
    anchor_keys = jnp.dot(selector, key_rows, preferred_element_type=jnp.float32)
    anchor_vals = jnp.dot(selector, value_rows, preferred_element_type=jnp.float32)
    initial = (
        jnp.full((kv_local, group_size, block_rows), -jnp.inf, jnp.float32),
        jnp.zeros((kv_local, group_size, block_rows), jnp.float32),
        jnp.zeros((kv_local, group_size, block_rows, head_dim), jnp.float32),
    )
    own_bias = jnp.zeros((kv_local, group_size), jnp.float32)
    softmax_state = absorb(initial, query_heads, key_rows, value_rows, own_bias, score_scale)
    bit_list = list(range(level_count))
    carried_keys = anchor_keys.astype(jnp.bfloat16)
    carried_vals = anchor_vals.astype(jnp.bfloat16)
    for bit_level in bit_list:
        partner_keys, partner_vals, more_keys, more_vals = partner_2(
            (key_rows, value_rows, carried_keys, carried_vals), "seq", bit_level
        )
        carried_keys = (carried_keys.astype(jnp.float32) + more_keys.astype(jnp.float32)).astype(
            jnp.bfloat16
        )
        carried_vals = (carried_vals.astype(jnp.float32) + more_vals.astype(jnp.float32)).astype(
            jnp.bfloat16
        )
        partner = jnp.bitwise_xor(block_index, 1 << bit_level)
        chosen = (partners[0] == partner).astype(jnp.float32)
        softmax_state = absorb(
            softmax_state,
            query_heads,
            partner_keys,
            partner_vals,
            jnp.sum(level_bias * chosen[None, :], axis=1).reshape(kv_local, group_size),
            score_scale,
        )
    softmax_state = absorb(
        softmax_state,
        query_heads,
        carried_keys,
        carried_vals,
        anchor_bias.reshape(kv_local, group_size),
        score_scale,
    )
    running_max, running_sum, weighted = softmax_state
    result = (
        (weighted / running_sum[..., None])
        .transpose(2, 0, 1, 3)
        .reshape(block_rows, -1)
        .astype(jnp.bfloat16)
    )
    return lax.all_to_all(result, "head", split_axis=0, concat_axis=1, tiled=True)


def solution(mesh):
    in_specs = (
        P(("seq", "head"), None),
        P(("seq", "head"), None),
        P(("seq", "head"), None),
        P("head", None),
        P("head"),
        P("seq", None),
        P(),
    )
    out_specs = P(("seq", "head"), None)
    return jax.shard_map(
        on_device, mesh=mesh, in_specs=in_specs, out_specs=out_specs, check_vma=False
    )
```

profile of v0, /device:TPU:96, one launch (start us, length us, event | category | flops | bytes accessed | tf_op | source)
XLA Modules:
  0.0 209.3 jit_solution(2618310160390596221)
XLA Ops:
  1.6 6.9 %all-to-all-start = ((bf16[64,8,128]{2,0,1:T(8,128)(2,1)}), bf16[64,8,128]{2,0,1:T(8,128)(2,1)S(1)}, u32[]{:S(2)}, u32[]{:S(2)}) async-start(bf16[64,8,128]{2,0,1:T(8,128)(2,1)} %copy_bitcast_fusion.2), calls=%async_computation | async-start | bytes 262144 | tf_op jit(solution)/shard_map/all_to_all | solution.py:40
  16.4 4.3 %all-to-all-start.2 = ((bf16[64,8,128]{2,0,1:T(8,128)(2,1)}), bf16[64,8,128]{2,0,1:T(8,128)(2,1)S(1)}, u32[]{:S(2)}, u32[]{:S(2)}) async-start(bf16[64,8,128]{2,0,1:T(8,128)(2,1)} %copy_bitcast_fusion.1), calls=%async_computation.2 | async-start | bytes 262144 | tf_op jit(solution)/shard_map/all_to_all | solution.py:41
  20.7 13.0 %collective-permute-start.10 = (bf16[512,128]{1,0:T(8,128)(2,1)S(1)}, bf16[512,128]{1,0:T(8,128)(2,1)S(1)}, u32[]{:S(2)}, u32[]{:S(2)}) collective-permute-start(bf16[512,128]{1,0:T(8,128)(2,1)S(1)} %bitcast.408), channel_id=1, source_target_pairs={{0,256},{8,264},{16,272},{24,280},{32,288},{40,296},{48,304},{56,3... | collective-permute-start | bytes 393224 | tf_op jit(solution)/shard_map/ppermute | solution.py:10
  33.7 4.3 %collective-permute-start.8 = (bf16[512,128]{1,0:T(8,128)(2,1)S(1)}, bf16[512,128]{1,0:T(8,128)(2,1)S(1)}, u32[]{:S(2)}, u32[]{:S(2)}) collective-permute-start(bf16[512,128]{1,0:T(8,128)(2,1)S(1)} %bitcast.409), channel_id=1, source_target_pairs={{0,128},{8,136},{16,144},{24,152},{32,160},{40,168},{48,176},{56,1... | collective-permute-start | bytes 393224 | tf_op jit(solution)/shard_map/ppermute | solution.py:10
  38.0 3.4 %collective-permute-start.6 = (bf16[512,128]{1,0:T(8,128)(2,1)S(1)}, bf16[512,128]{1,0:T(8,128)(2,1)S(1)}, u32[]{:S(2)}, u32[]{:S(2)}) collective-permute-start(bf16[512,128]{1,0:T(8,128)(2,1)S(1)} %bitcast.410), channel_id=1, source_target_pairs={{0,64},{8,72},{16,80},{24,88},{32,96},{40,104},{48,112},{56,120},{... | collective-permute-start | bytes 393224 | tf_op jit(solution)/shard_map/ppermute | solution.py:10
  47.1 7.2 %all-to-all-start.1 = ((bf16[64,8,512]{2,0,1:T(8,128)(2,1)}), bf16[64,8,512]{2,0,1:T(8,128)(2,1)S(1)}, u32[]{:S(2)}, u32[]{:S(2)}) async-start(bf16[64,8,512]{2,0,1:T(8,128)(2,1)} %bitcast.405), calls=%async_computation.1 | async-start | bytes 1048576 | tf_op jit(solution)/shard_map/all_to_all | solution.py:39
  60.9 3.1 %collective-permute-done.13 = bf16[64,128]{1,0:T(8,128)(2,1)S(1)} collective-permute-done((bf16[64,128]{1,0:T(8,128)(2,1)S(1)}, bf16[64,128]{1,0:T(8,128)(2,1)S(1)}, u32[]{:S(2)}, u32[]{:S(2)}) %collective-permute-start.13) | collective-permute-done | bytes 16416 | tf_op jit(solution)/shard_map/ppermute | solution.py:10
  80.9 3.4 %collective-permute-start.15 = (bf16[64,128]{1,0:T(8,128)(2,1)S(1)}, bf16[64,128]{1,0:T(8,128)(2,1)S(1)}, u32[]{:S(2)}, u32[]{:S(2)}) collective-permute-start(bf16[64,128]{1,0:T(8,128)(2,1)S(1)} %add_convert_fusion.9), channel_id=1, source_target_pairs={{0,64},{8,72},{16,80},{24,88},{32,96},{40,104},{48,112},{56,120},{... | collective-permute-start | bytes 49160 | tf_op jit(solution)/shard_map/ppermute | solution.py:10
  84.3 3.1 %collective-permute-done.15 = bf16[64,128]{1,0:T(8,128)(2,1)S(1)} collective-permute-done((bf16[64,128]{1,0:T(8,128)(2,1)S(1)}, bf16[64,128]{1,0:T(8,128)(2,1)S(1)}, u32[]{:S(2)}, u32[]{:S(2)}) %collective-permute-start.15) | collective-permute-done | bytes 16416 | tf_op jit(solution)/shard_map/ppermute | solution.py:10
  87.4 3.5 %collective-permute-start.21 = (bf16[64,128]{1,0:T(8,128)(2,1)S(1)}, bf16[64,128]{1,0:T(8,128)(2,1)S(1)}, u32[]{:S(2)}, u32[]{:S(2)}) collective-permute-start(bf16[64,128]{1,0:T(8,128)(2,1)S(1)} %add_convert_fusion.3), channel_id=1, source_target_pairs={{0,64},{8,72},{16,80},{24,88},{32,96},{40,104},{48,112},{56,120},{... | collective-permute-start | bytes 49160 | tf_op jit(solution)/shard_map/ppermute | solution.py:10
  90.9 3.0 %collective-permute-done.21 = bf16[64,128]{1,0:T(8,128)(2,1)S(1)} collective-permute-done((bf16[64,128]{1,0:T(8,128)(2,1)S(1)}, bf16[64,128]{1,0:T(8,128)(2,1)S(1)}, u32[]{:S(2)}, u32[]{:S(2)}) %collective-permute-start.21) | collective-permute-done | bytes 16416 | tf_op jit(solution)/shard_map/ppermute | solution.py:10
  93.9 5.4 %collective-permute-start.16 = (bf16[64,128]{1,0:T(8,128)(2,1)S(1)}, bf16[64,128]{1,0:T(8,128)(2,1)S(1)}, u32[]{:S(2)}, u32[]{:S(2)}) collective-permute-start(bf16[64,128]{1,0:T(8,128)(2,1)S(1)} %add_convert_fusion.8), channel_id=1, source_target_pairs={{0,128},{8,136},{16,144},{24,152},{32,160},{40,168},{48,176},{56,1... | collective-permute-start | bytes 49160 | tf_op jit(solution)/shard_map/ppermute | solution.py:10
  99.4 4.2 %collective-permute-done.16 = bf16[64,128]{1,0:T(8,128)(2,1)S(1)} collective-permute-done((bf16[64,128]{1,0:T(8,128)(2,1)S(1)}, bf16[64,128]{1,0:T(8,128)(2,1)S(1)}, u32[]{:S(2)}, u32[]{:S(2)}) %collective-permute-start.16) | collective-permute-done | bytes 16416 | tf_op jit(solution)/shard_map/ppermute | solution.py:10
  103.5 5.3 %collective-permute-start.22 = (bf16[64,128]{1,0:T(8,128)(2,1)S(1)}, bf16[64,128]{1,0:T(8,128)(2,1)S(1)}, u32[]{:S(2)}, u32[]{:S(2)}) collective-permute-start(bf16[64,128]{1,0:T(8,128)(2,1)S(1)} %add_convert_fusion.2), channel_id=1, source_target_pairs={{0,128},{8,136},{16,144},{24,152},{32,160},{40,168},{48,176},{56,1... | collective-permute-start | bytes 49160 | tf_op jit(solution)/shard_map/ppermute | solution.py:10
  108.9 4.2 %collective-permute-done.22 = bf16[64,128]{1,0:T(8,128)(2,1)S(1)} collective-permute-done((bf16[64,128]{1,0:T(8,128)(2,1)S(1)}, bf16[64,128]{1,0:T(8,128)(2,1)S(1)}, u32[]{:S(2)}, u32[]{:S(2)}) %collective-permute-start.22) | collective-permute-done | bytes 16416 | tf_op jit(solution)/shard_map/ppermute | solution.py:10
  118.5 3.3 %collective-permute-start.3 = (bf16[512,128]{1,0:T(8,128)(2,1)S(1)}, bf16[512,128]{1,0:T(8,128)(2,1)S(1)}, u32[]{:S(2)}, u32[]{:S(2)}) collective-permute-start(bf16[512,128]{1,0:T(8,128)(2,1)S(1)} %bitcast.418), channel_id=1, source_target_pairs={{0,16},{8,24},{16,0},{24,8},{32,48},{40,56},{48,32},{56,40},{64,80... | collective-permute-start | bytes 393224 | tf_op jit(solution)/shard_map/ppermute | solution.py:10
  126.2 3.3 %collective-permute-start.7 = (bf16[512,128]{1,0:T(8,128)(2,1)S(1)}, bf16[512,128]{1,0:T(8,128)(2,1)S(1)}, u32[]{:S(2)}, u32[]{:S(2)}) collective-permute-start(bf16[512,128]{1,0:T(8,128)(2,1)S(1)} %bitcast.420), channel_id=1, source_target_pairs={{0,64},{8,72},{16,80},{24,88},{32,96},{40,104},{48,112},{56,120},{... | collective-permute-start | bytes 393224 | tf_op jit(solution)/shard_map/ppermute | solution.py:10
  130.2 5.6 %collective-permute-start.9 = (bf16[512,128]{1,0:T(8,128)(2,1)S(1)}, bf16[512,128]{1,0:T(8,128)(2,1)S(1)}, u32[]{:S(2)}, u32[]{:S(2)}) collective-permute-start(bf16[512,128]{1,0:T(8,128)(2,1)S(1)} %bitcast.421), channel_id=1, source_target_pairs={{0,128},{8,136},{16,144},{24,152},{32,160},{40,168},{48,176},{56,1... | collective-permute-start | bytes 393224 | tf_op jit(solution)/shard_map/ppermute | solution.py:10
  141.4 10.2 %collective-permute-done.17 = bf16[64,128]{1,0:T(8,128)(2,1)S(1)} collective-permute-done((bf16[64,128]{1,0:T(8,128)(2,1)S(1)}, bf16[64,128]{1,0:T(8,128)(2,1)S(1)}, u32[]{:S(2)}, u32[]{:S(2)}) %collective-permute-start.17) | collective-permute-done | bytes 16416 | tf_op jit(solution)/shard_map/ppermute | solution.py:10
  151.6 9.8 %collective-permute-start.11 = (bf16[512,128]{1,0:T(8,128)(2,1)S(1)}, bf16[512,128]{1,0:T(8,128)(2,1)S(1)}, u32[]{:S(2)}, u32[]{:S(2)}) collective-permute-start(bf16[512,128]{1,0:T(8,128)(2,1)S(1)} %bitcast.422), channel_id=1, source_target_pairs={{0,256},{8,264},{16,272},{24,280},{32,288},{40,296},{48,304},{56,3... | collective-permute-start | bytes 393224 | tf_op jit(solution)/shard_map/ppermute | solution.py:10
  171.7 5.2 %collective-permute-start.23 = (bf16[64,128]{1,0:T(8,128)(2,1)S(1)}, bf16[64,128]{1,0:T(8,128)(2,1)S(1)}, u32[]{:S(2)}, u32[]{:S(2)}) collective-permute-start(bf16[64,128]{1,0:T(8,128)(2,1)S(1)} %add_convert_fusion.1), channel_id=1, source_target_pairs={{0,256},{8,264},{16,272},{24,280},{32,288},{40,296},{48,304},{56,3... | collective-permute-start | bytes 49160 | tf_op jit(solution)/shard_map/ppermute | solution.py:10
  181.3 4.8 %collective-permute-done.23 = bf16[64,128]{1,0:T(8,128)(2,1)S(1)} collective-permute-done((bf16[64,128]{1,0:T(8,128)(2,1)S(1)}, bf16[64,128]{1,0:T(8,128)(2,1)S(1)}, u32[]{:S(2)}, u32[]{:S(2)}) %collective-permute-start.23) | collective-permute-done | bytes 16416 | tf_op jit(solution)/shard_map/ppermute | solution.py:10
  186.4 3.4 %fusion.98 = bf16[512,1,4,128]{3,0,2,1:T(8,128)(2,1)S(1)} fusion(f32[4,512,128]{2,1,0:T(8,128)S(1)} %fusion.104, f32[4,512,128]{2,1,0:T(8,128)S(1)} %fusion.42, f32[4,512,128]{2,1,0:T(8,128)S(1)} %fusion.40, f32[4,512,128]{2,1,0:T(8,128)S(1)} %fusion.38, f32[4,512,128]{2,1,0:T(8,128)S(1)} %fusion.36, f32[4,512,128]{2,1,0:T(8,128)S(1)} %fusion.34, ...), kind=kOutput, calls=%fused_computation.80 | convolution fusion | flops 276561920 | bytes 12255248 | tf_op jit(solution)/shard_map/kgts,skd->kgtd/dot_general | solution.py:27
  190.5 18.0 %all_to_all.64 = bf16[8,64,512]{2,1,0:T(8,128)(2,1)S(1)} all-to-all(bf16[8,64,512]{2,1,0:T(8,128)(2,1)S(1)} %convert_element_type.213), channel_id=1, replica_groups=mesh['seq'=64,'head'=8] {'head'}, dimensions={0} | all-to-all | bytes 1048576 | tf_op jit(solution)/shard_map/all_to_all | solution.py:100
  (80 shorter events, 71.1 us)
Async XLA Ops:
  1.6 14.8 %all-to-all-start = ((bf16[64,8,128]{2,0,1:T(8,128)(2,1)}), bf16[64,8,128]{2,0,1:T(8,128)(2,1)S(1)}, u32[]{:S(2)}, u32[]{:S(2)}) async-start(bf16[64,8,128]{2,0,1:T(8,128)(2,1)} %copy_bitcast_fusion.2), calls=%async_computation | async-start | bytes 262144 | tf_op jit(solution)/shard_map/all_to_all | solution.py:40
  16.4 30.7 %all-to-all-start.2 = ((bf16[64,8,128]{2,0,1:T(8,128)(2,1)}), bf16[64,8,128]{2,0,1:T(8,128)(2,1)S(1)}, u32[]{:S(2)}, u32[]{:S(2)}) async-start(bf16[64,8,128]{2,0,1:T(8,128)(2,1)} %copy_bitcast_fusion.1), calls=%async_computation.2 | async-start | bytes 262144 | tf_op jit(solution)/shard_map/all_to_all | solution.py:41
  20.7 95.1 %collective-permute-start.10 = (bf16[512,128]{1,0:T(8,128)(2,1)S(1)}, bf16[512,128]{1,0:T(8,128)(2,1)S(1)}, u32[]{:S(2)}, u32[]{:S(2)}) collective-permute-start(bf16[512,128]{1,0:T(8,128)(2,1)S(1)} %bitcast.408), channel_id=1, source_target_pairs={{0,256},{8,264},{16,272},{24,280},{32,288},{40,296},{48,304},{56,3... | collective-permute-start | bytes 393224 | tf_op jit(solution)/shard_map/ppermute | solution.py:10
  33.7 84.7 %collective-permute-start.8 = (bf16[512,128]{1,0:T(8,128)(2,1)S(1)}, bf16[512,128]{1,0:T(8,128)(2,1)S(1)}, u32[]{:S(2)}, u32[]{:S(2)}) collective-permute-start(bf16[512,128]{1,0:T(8,128)(2,1)S(1)} %bitcast.409), channel_id=1, source_target_pairs={{0,128},{8,136},{16,144},{24,152},{32,160},{40,168},{48,176},{56,1... | collective-permute-start | bytes 393224 | tf_op jit(solution)/shard_map/ppermute | solution.py:10
  38.0 84.5 %collective-permute-start.6 = (bf16[512,128]{1,0:T(8,128)(2,1)S(1)}, bf16[512,128]{1,0:T(8,128)(2,1)S(1)}, u32[]{:S(2)}, u32[]{:S(2)}) collective-permute-start(bf16[512,128]{1,0:T(8,128)(2,1)S(1)} %bitcast.410), channel_id=1, source_target_pairs={{0,64},{8,72},{16,80},{24,88},{32,96},{40,104},{48,112},{56,120},{... | collective-permute-start | bytes 393224 | tf_op jit(solution)/shard_map/ppermute | solution.py:10
  41.4 84.8 %collective-permute-start.4 = (bf16[512,128]{1,0:T(8,128)(2,1)S(1)}, bf16[512,128]{1,0:T(8,128)(2,1)S(1)}, u32[]{:S(2)}, u32[]{:S(2)}) collective-permute-start(bf16[512,128]{1,0:T(8,128)(2,1)S(1)} %bitcast.411), channel_id=1, source_target_pairs={{0,32},{8,40},{16,48},{24,56},{32,0},{40,8},{48,16},{56,24},{64,96... | collective-permute-start | bytes 393224 | tf_op jit(solution)/shard_map/ppermute | solution.py:10
  45.2 10.0 %collective-permute-start.12 = (bf16[64,128]{1,0:T(8,128)(2,1)S(1)}, bf16[64,128]{1,0:T(8,128)(2,1)S(1)}, u32[]{:S(2)}, u32[]{:S(2)}) collective-permute-start(bf16[64,128]{1,0:T(8,128)(2,1)S(1)} %convolution_convert_fusion.1), channel_id=1, source_target_pairs={{0,8},{8,0},{16,24},{24,16},{32,40},{40,32},{48,56},{56,48},{64,72... | collective-permute-start | bytes 49160 | tf_op jit(solution)/shard_map/ppermute | solution.py:10
  47.1 68.5 %all-to-all-start.1 = ((bf16[64,8,512]{2,0,1:T(8,128)(2,1)}), bf16[64,8,512]{2,0,1:T(8,128)(2,1)S(1)}, u32[]{:S(2)}, u32[]{:S(2)}) async-start(bf16[64,8,512]{2,0,1:T(8,128)(2,1)} %bitcast.405), calls=%async_computation.1 | async-start | bytes 1048576 | tf_op jit(solution)/shard_map/all_to_all | solution.py:39
  58.3 5.7 %collective-permute-start.13 = (bf16[64,128]{1,0:T(8,128)(2,1)S(1)}, bf16[64,128]{1,0:T(8,128)(2,1)S(1)}, u32[]{:S(2)}, u32[]{:S(2)}) collective-permute-start(bf16[64,128]{1,0:T(8,128)(2,1)S(1)} %add_convert_fusion.11), channel_id=1, source_target_pairs={{0,16},{8,24},{16,0},{24,8},{32,48},{40,56},{48,32},{56,40},{64,80... | collective-permute-start | bytes 49160 | tf_op jit(solution)/shard_map/ppermute | solution.py:10
  64.0 5.6 %collective-permute-start.19 = (bf16[64,128]{1,0:T(8,128)(2,1)S(1)}, bf16[64,128]{1,0:T(8,128)(2,1)S(1)}, u32[]{:S(2)}, u32[]{:S(2)}) collective-permute-start(bf16[64,128]{1,0:T(8,128)(2,1)S(1)} %add_convert_fusion.5), channel_id=1, source_target_pairs={{0,16},{8,24},{16,0},{24,8},{32,48},{40,56},{48,32},{56,40},{64,80... | collective-permute-start | bytes 49160 | tf_op jit(solution)/shard_map/ppermute | solution.py:10
  80.9 6.5 %collective-permute-start.15 = (bf16[64,128]{1,0:T(8,128)(2,1)S(1)}, bf16[64,128]{1,0:T(8,128)(2,1)S(1)}, u32[]{:S(2)}, u32[]{:S(2)}) collective-permute-start(bf16[64,128]{1,0:T(8,128)(2,1)S(1)} %add_convert_fusion.9), channel_id=1, source_target_pairs={{0,64},{8,72},{16,80},{24,88},{32,96},{40,104},{48,112},{56,120},{... | collective-permute-start | bytes 49160 | tf_op jit(solution)/shard_map/ppermute | solution.py:10
  87.4 6.5 %collective-permute-start.21 = (bf16[64,128]{1,0:T(8,128)(2,1)S(1)}, bf16[64,128]{1,0:T(8,128)(2,1)S(1)}, u32[]{:S(2)}, u32[]{:S(2)}) collective-permute-start(bf16[64,128]{1,0:T(8,128)(2,1)S(1)} %add_convert_fusion.3), channel_id=1, source_target_pairs={{0,64},{8,72},{16,80},{24,88},{32,96},{40,104},{48,112},{56,120},{... | collective-permute-start | bytes 49160 | tf_op jit(solution)/shard_map/ppermute | solution.py:10
  93.9 9.6 %collective-permute-start.16 = (bf16[64,128]{1,0:T(8,128)(2,1)S(1)}, bf16[64,128]{1,0:T(8,128)(2,1)S(1)}, u32[]{:S(2)}, u32[]{:S(2)}) collective-permute-start(bf16[64,128]{1,0:T(8,128)(2,1)S(1)} %add_convert_fusion.8), channel_id=1, source_target_pairs={{0,128},{8,136},{16,144},{24,152},{32,160},{40,168},{48,176},{56,1... | collective-permute-start | bytes 49160 | tf_op jit(solution)/shard_map/ppermute | solution.py:10
  103.5 9.5 %collective-permute-start.22 = (bf16[64,128]{1,0:T(8,128)(2,1)S(1)}, bf16[64,128]{1,0:T(8,128)(2,1)S(1)}, u32[]{:S(2)}, u32[]{:S(2)}) collective-permute-start(bf16[64,128]{1,0:T(8,128)(2,1)S(1)} %add_convert_fusion.2), channel_id=1, source_target_pairs={{0,128},{8,136},{16,144},{24,152},{32,160},{40,168},{48,176},{56,1... | collective-permute-start | bytes 49160 | tf_op jit(solution)/shard_map/ppermute | solution.py:10
  113.1 17.1 %collective-permute-start.2 = (bf16[512,128]{1,0:T(8,128)(2,1)S(1)}, bf16[512,128]{1,0:T(8,128)(2,1)S(1)}, u32[]{:S(2)}, u32[]{:S(2)}) collective-permute-start(bf16[512,128]{1,0:T(8,128)(2,1)S(1)} %bitcast.413), channel_id=1, source_target_pairs={{0,16},{8,24},{16,0},{24,8},{32,48},{40,56},{48,32},{56,40},{64,80... | collective-permute-start | bytes 393224 | tf_op jit(solution)/shard_map/ppermute | solution.py:10
  115.8 21.4 %collective-permute-start = (bf16[512,128]{1,0:T(8,128)(2,1)S(1)}, bf16[512,128]{1,0:T(8,128)(2,1)S(1)}, u32[]{:S(2)}, u32[]{:S(2)}) collective-permute-start(bf16[512,128]{1,0:T(8,128)(2,1)S(1)} %bitcast.414), channel_id=1, source_target_pairs={{0,8},{8,0},{16,24},{24,16},{32,40},{40,32},{48,56},{56,48},{64,72... | collective-permute-start | bytes 393224 | tf_op jit(solution)/shard_map/ppermute | solution.py:10
  118.5 50.2 %collective-permute-start.3 = (bf16[512,128]{1,0:T(8,128)(2,1)S(1)}, bf16[512,128]{1,0:T(8,128)(2,1)S(1)}, u32[]{:S(2)}, u32[]{:S(2)}) collective-permute-start(bf16[512,128]{1,0:T(8,128)(2,1)S(1)} %bitcast.418), channel_id=1, source_target_pairs={{0,16},{8,24},{16,0},{24,8},{32,48},{40,56},{48,32},{56,40},{64,80... | collective-permute-start | bytes 393224 | tf_op jit(solution)/shard_map/ppermute | solution.py:10
  122.5 49.2 %collective-permute-start.5 = (bf16[512,128]{1,0:T(8,128)(2,1)S(1)}, bf16[512,128]{1,0:T(8,128)(2,1)S(1)}, u32[]{:S(2)}, u32[]{:S(2)}) collective-permute-start(bf16[512,128]{1,0:T(8,128)(2,1)S(1)} %bitcast.419), channel_id=1, source_target_pairs={{0,32},{8,40},{16,48},{24,56},{32,0},{40,8},{48,16},{56,24},{64,96... | collective-permute-start | bytes 393224 | tf_op jit(solution)/shard_map/ppermute | solution.py:10
  126.2 51.8 %collective-permute-start.7 = (bf16[512,128]{1,0:T(8,128)(2,1)S(1)}, bf16[512,128]{1,0:T(8,128)(2,1)S(1)}, u32[]{:S(2)}, u32[]{:S(2)}) collective-permute-start(bf16[512,128]{1,0:T(8,128)(2,1)S(1)} %bitcast.420), channel_id=1, source_target_pairs={{0,64},{8,72},{16,80},{24,88},{32,96},{40,104},{48,112},{56,120},{... | collective-permute-start | bytes 393224 | tf_op jit(solution)/shard_map/ppermute | solution.py:10
  130.2 48.9 %collective-permute-start.9 = (bf16[512,128]{1,0:T(8,128)(2,1)S(1)}, bf16[512,128]{1,0:T(8,128)(2,1)S(1)}, u32[]{:S(2)}, u32[]{:S(2)}) collective-permute-start(bf16[512,128]{1,0:T(8,128)(2,1)S(1)} %bitcast.421), channel_id=1, source_target_pairs={{0,128},{8,136},{16,144},{24,152},{32,160},{40,168},{48,176},{56,1... | collective-permute-start | bytes 393224 | tf_op jit(solution)/shard_map/ppermute | solution.py:10
  137.2 14.4 %collective-permute-start.17 = (bf16[64,128]{1,0:T(8,128)(2,1)S(1)}, bf16[64,128]{1,0:T(8,128)(2,1)S(1)}, u32[]{:S(2)}, u32[]{:S(2)}) collective-permute-start(bf16[64,128]{1,0:T(8,128)(2,1)S(1)} %add_convert_fusion.7), channel_id=1, source_target_pairs={{0,256},{8,264},{16,272},{24,280},{32,288},{40,296},{48,304},{56,3... | collective-permute-start | bytes 49160 | tf_op jit(solution)/shard_map/ppermute | solution.py:10
  151.6 28.6 %collective-permute-start.11 = (bf16[512,128]{1,0:T(8,128)(2,1)S(1)}, bf16[512,128]{1,0:T(8,128)(2,1)S(1)}, u32[]{:S(2)}, u32[]{:S(2)}) collective-permute-start(bf16[512,128]{1,0:T(8,128)(2,1)S(1)} %bitcast.422), channel_id=1, source_target_pairs={{0,256},{8,264},{16,272},{24,280},{32,288},{40,296},{48,304},{56,3... | collective-permute-start | bytes 393224 | tf_op jit(solution)/shard_map/ppermute | solution.py:10
  168.7 17.7 %collective-permute-start.1 = (bf16[512,128]{1,0:T(8,128)(2,1)S(1)}, bf16[512,128]{1,0:T(8,128)(2,1)S(1)}, u32[]{:S(2)}, u32[]{:S(2)}) collective-permute-start(bf16[512,128]{1,0:T(8,128)(2,1)S(1)} %bitcast.424), channel_id=1, source_target_pairs={{0,8},{8,0},{16,24},{24,16},{32,40},{40,32},{48,56},{56,48},{64,72... | collective-permute-start | bytes 393224 | tf_op jit(solution)/shard_map/ppermute | solution.py:10
  171.7 14.3 %collective-permute-start.23 = (bf16[64,128]{1,0:T(8,128)(2,1)S(1)}, bf16[64,128]{1,0:T(8,128)(2,1)S(1)}, u32[]{:S(2)}, u32[]{:S(2)}) collective-permute-start(bf16[64,128]{1,0:T(8,128)(2,1)S(1)} %add_convert_fusion.1), channel_id=1, source_target_pairs={{0,256},{8,264},{16,272},{24,280},{32,288},{40,296},{48,304},{56,3... | collective-permute-start | bytes 49160 | tf_op jit(solution)/shard_map/ppermute | solution.py:10
  (5 other events, 36.7 us)
where the time goes:
time: 210 us; the launch traced here: 209 us
  starting transfers between devices  114 us (54%)
  waiting for transfers between devices  44.7 us (21%)
  blocking collectives  18 us (9%)
  matrix products  17.9 us (9%)
  other arithmetic  7.69 us (4%)
  local copies, waits for them, and re-layouts  6.61 us (3%)
    ppermute x24, starting transfers between devices, partner_2(): lax.ppermute(value, axis, [(i, i ^ 1 << stride) for i in range(lax.axis_s...  95.4 us
    ppermute x24, waiting for transfers between devices, partner_2(): lax.ppermute(value, axis, [(i, i ^ 1 << stride) for i in range(lax.axis_s...  41.7 us
    all_to_all x1, blocking collectives, on_device(): lax.all_to_all(result, 'head', split_axis=0, concat_axis=1, tiled=True)  18 us
    dot_general x8, matrix products, absorb(): jnp.einsum('kgts,skd->kgtd', weights.astype(jnp.bfloat16), value_heads, p...  10.8 us
    all_to_all x1, starting transfers between devices, on_device(): lax.all_to_all(queries, 'head', split_axis=1, concat_axis=0, tiled=True)  7.22 us
    all_to_all x1, starting transfers between devices, on_device(): lax.all_to_all(keys, 'head', split_axis=1, concat_axis=0, tiled=True)  6.93 us
    reduce_sum x5, other arithmetic, absorb(): running_sum = running_sum * rescale + jnp.sum(weights, axis=-1)  6 us
    dot_general x8, matrix products, absorb(): jnp.einsum('tkgd,skd->kgts', query_heads, key_heads, preferred_element_ty...  5.4 us
  transfers between devices with their start and end apart: 27, of which 12 were waited for; matrix products, arithmetic and copies ran while one was open for 12% of the time, Pallas kernels for 0%

commit v1 on v0

v1 whole, which is shorter than its diff:
```python
import functools
import math

import jax
import jax.numpy as jnp
from jax import lax
from jax.experimental import pallas as pl
from jax.experimental.pallas import tpu as pltpu
from jax.sharding import PartitionSpec as P

HD = 128
LOG2E = math.log2(math.e)


def swap(value, bit):
    return lax.ppermute(value, "seq", [(i, i ^ (1 << bit)) for i in range(lax.axis_size("seq"))])


def attend_kernel(count, first, final, bias_ref, q_ref, *refs):
    kv_refs, refs = refs[:count], refs[count:]
    if not first:
        acc_in, ml_in, refs = refs[0], refs[1], refs[2:]
    head = pl.program_id(0)
    scale = HD**-0.5 * LOG2E
    rows = q_ref.shape[0]
    tile = 256
    for start in range(0, rows, tile):
        part = pl.ds(start, tile)
        query = q_ref[part, :]
        scores, top = [], None
        for j in range(count):
            s = lax.dot_general(
                query, kv_refs[j][:, :HD], (((1,), (1,)), ((), ())), preferred_element_type=jnp.float32
            )
            bias = bias_ref[j, head] * LOG2E
            most = jnp.max(s, axis=-1, keepdims=True) * scale + bias
            top = most if top is None else jnp.maximum(top, most)
            scores.append((s, bias))
        if not first:
            old_top = ml_in[0, part, 0:1]
            top = jnp.maximum(top, old_top)
        total = None
        for j in range(count):
            s, bias = scores[j]
            weights = jnp.exp2(s * scale - (top - bias)).astype(jnp.bfloat16)
            value = kv_refs[j][:, HD:]
            widened = jnp.concatenate([value, jnp.ones_like(value)], axis=1)
            update = jnp.dot(weights, widened, preferred_element_type=jnp.float32)
            total = update if total is None else total + update
        acc, summed = total[:, :HD], total[:, HD:]
        if not first:
            rescale = jnp.exp2(old_top - top)
            acc = acc + acc_in[0, part, :] * rescale
            summed = summed + ml_in[0, part, 1:2] * rescale
        if final:
            refs[0][part, :] = (acc / summed).astype(jnp.bfloat16)
        else:
            refs[0][0, part, :] = acc
            refs[1][0, part, 0:1] = top
            refs[1][0, part, 1:2] = summed[:, 0:1]


def attend(state, queries, blocks, biases, final=False):
    rows, width = queries.shape
    heads = biases.shape[1]
    count, first = len(blocks), state is None
    acc_spec = pl.BlockSpec((1, rows, HD), lambda h: (h, 0, 0))
    ml_spec = pl.BlockSpec((1, rows, 2), lambda h: (h, 0, 0))
    q_spec = pl.BlockSpec((rows, HD), lambda h: (0, h))
    in_specs = [pl.BlockSpec(memory_space=pltpu.SMEM), q_spec]
    in_specs += [pl.BlockSpec(b.shape, lambda h: (0, 0)) for b in blocks]
    args = [biases, queries, *blocks]
    if not first:
        in_specs += [acc_spec, ml_spec]
        args += list(state)
    if final:
        out_shape = jax.ShapeDtypeStruct((rows, heads * HD), jnp.bfloat16)
        out_specs = q_spec
    else:
        out_shape = (
            jax.ShapeDtypeStruct((heads, rows, HD), jnp.float32),
            jax.ShapeDtypeStruct((heads, rows, 2), jnp.float32),
        )
        out_specs = (acc_spec, ml_spec)
    return pl.pallas_call(
        functools.partial(attend_kernel, count, first, final),
        grid=(heads,),
        in_specs=in_specs,
        out_specs=out_specs,
        out_shape=out_shape,
        compiler_params=pltpu.CompilerParams(vmem_limit_bytes=48 * 1024 * 1024),
    )(*args)


def on_device(queries, keys, values, level_bias, anchor_bias, partners, anchor_positions):
    tokens = queries.shape[0]
    shards = lax.axis_size("head")
    block_index = lax.axis_index("seq")
    bits = lax.axis_size("seq").bit_length() - 1

    def by_head(array):
        return array.reshape(tokens, shards, -1).transpose(1, 0, 2)

    def to_heads(array):
        gathered = lax.all_to_all(array, "head", split_axis=0, concat_axis=0, tiled=True)
        return gathered.reshape(shards * tokens, -1)

    kv_shard = jnp.concatenate([by_head(keys), by_head(values)], axis=2)
    far_shard = swap(kv_shard, bits - 1)
    qkv = to_heads(jnp.concatenate([by_head(queries), kv_shard], axis=2))
    q_width = queries.shape[1] // shards
    q, kv = qkv[:, :q_width], qkv[:, q_width:]

    token_index = block_index * kv.shape[0] + jnp.arange(kv.shape[0], dtype=jnp.int32)
    selector = (anchor_positions[:, None] == token_index[None, :]).astype(jnp.bfloat16)
    anchors = jnp.dot(selector, kv, preferred_element_type=jnp.float32).astype(jnp.bfloat16)

    others = [swap(kv, bit) for bit in range(bits - 1)]
    for bit in range(bits):
        anchors = anchors + swap(anchors, bit)
    far = to_heads(far_shard)

    block_bias = [jnp.zeros_like(anchor_bias)]
    for bit in range(bits):
        chosen = (partners[0] == jnp.bitwise_xor(block_index, 1 << bit)).astype(jnp.float32)
        block_bias.append(jnp.sum(level_bias * chosen[None, :], axis=1))
    block_bias.append(anchor_bias)
    bias = jnp.stack(block_bias)

    state = attend(None, q, [kv, others[0], others[1]], bias[0:3])
    state = attend(state, q, [others[2], others[3]], bias[3:5])
    state = attend(state, q, [far], bias[6:7])
    result = attend(state, q, [others[4], anchors], jnp.stack([bias[5], bias[7]]), final=True)
    return lax.all_to_all(result, "head", split_axis=0, concat_axis=1, tiled=True)


def solution(mesh):
    in_specs = (
        P(("seq", "head"), None),
        P(("seq", "head"), None),
        P(("seq", "head"), None),
        P("head", None),
        P("head"),
        P("seq", None),
        P(),
    )
    out_specs = P(("seq", "head"), None)
    return jax.shard_map(
        on_device, mesh=mesh, in_specs=in_specs, out_specs=out_specs, check_vma=False
    )
```

time: 210 us -> 161 us (0.77)
  starting transfers between devices: 114 us -> 53.6 us
  Pallas kernels: 0 us -> 25.5 us
  matrix products: 17.9 us -> 0.21 us
  waiting for transfers between devices: 44.7 us -> 58.1 us
  other arithmetic: 7.69 us -> 1.98 us
  local copies, waits for them, and re-layouts: 6.61 us -> 2.11 us
    ppermute x24 -> x12, starting transfers between devices: 95.4 us -> 42.7 us  [swap(): lax.ppermute(value, 'seq', [(i, i ^ 1 << bit) for i in range(lax.axis_siz...]
    pallas_call x0 -> x4, Pallas kernels: none -> 25.5 us  [attend(): pl.pallas_call(functools.partial(attend_kernel, count, first, final), gri...]
    dot_general x18 -> x1, matrix products: 17.9 us -> 0.21 us  [on_device(): jnp.dot(selector, kv, preferred_element_type=jnp.float32)]
    all_to_all x3 -> x2, waiting for transfers between devices: 2.93 us -> 13.3 us  [to_heads(): lax.all_to_all(array, 'head', split_axis=0, concat_axis=0, tiled=True)]
    all_to_all x3 -> x2, starting transfers between devices: 18.5 us -> 10.9 us  [to_heads(): lax.all_to_all(array, 'head', split_axis=0, concat_axis=0, tiled=True)]
    reduce_sum x6 -> x1, other arithmetic: 6.86 us -> 0.19 us  [on_device(): block_bias.append(jnp.sum(level_bias * chosen[None, :], axis=1))]
    all_to_all x3 -> x0, local copies, waits for them, and re-layouts: 4.12 us -> none  [the longest x1 1.88 us: on_device(): lax.all_to_all(queries, 'head', split_axis=1, concat_axis=0, tiled=True)]
    ppermute x24 -> x12, waiting for transfers between devices: 41.7 us -> 44.8 us  [swap(): lax.ppermute(value, 'seq', [(i, i ^ 1 << bit) for i in range(lax.axis_siz...]
  transfers between devices with their start and end apart: 27 -> 14, of which waited for: 12 -> 6; matrix products, arithmetic and copies ran while one was open for 12% -> 1% of each run, Pallas kernels for 0% -> 12%
where the time goes in v1:
time: 161 us; the launch traced here: 160 us
  waiting for transfers between devices  58.1 us (36%)
  starting transfers between devices  53.6 us (33%)
  Pallas kernels  25.5 us (16%)
  blocking collectives  18.3 us (11%)
  local copies, waits for them, and re-layouts  2.11 us (1%)
  other arithmetic  1.98 us (1%)
    ppermute x12, waiting for transfers between devices, swap(): lax.ppermute(value, 'seq', [(i, i ^ 1 << bit) for i in range(lax.axis_siz...  44.8 us
    ppermute x12, starting transfers between devices, swap(): lax.ppermute(value, 'seq', [(i, i ^ 1 << bit) for i in range(lax.axis_siz...  42.7 us
    pallas_call x4, Pallas kernels, attend(): pl.pallas_call(functools.partial(attend_kernel, count, first, final), gri...  25.5 us
    all_to_all x1, blocking collectives, on_device(): lax.all_to_all(result, 'head', split_axis=0, concat_axis=1, tiled=True)  18.3 us
    all_to_all x2, waiting for transfers between devices, to_heads(): lax.all_to_all(array, 'head', split_axis=0, concat_axis=0, tiled=True)  13.3 us
    all_to_all x2, starting transfers between devices, to_heads(): lax.all_to_all(array, 'head', split_axis=0, concat_axis=0, tiled=True)  10.9 us
  transfers between devices with their start and end apart: 14, of which 6 were waited for; matrix products, arithmetic and copies ran while one was open for 1% of the time, Pallas kernels for 12%

profile of v1, /device:TPU:96, one launch (start us, length us, event | category | flops | bytes accessed | tf_op | source)
XLA Modules:
  0.0 160.1 jit_solution(6536621074429999268)
XLA Ops:
  2.2 7.1 %all-to-all-start = ((bf16[8,64,768]{2,1,0:T(8,128)(2,1)}), bf16[8,64,768]{2,1,0:T(8,128)(2,1)S(1)}, u32[]{:S(2)}, u32[]{:S(2)}) async-start(bf16[8,64,768]{2,1,0:T(8,128)(2,1)} %pad_maximum_fusion), calls=%async_computation | async-start | bytes 1572864 | tf_op jit(solution)/shard_map/all_to_all | solution.py:105
  9.3 13.3 %all-to-all-done = bf16[8,64,768]{2,1,0:T(8,128)(2,1)S(1)} async-done(((bf16[8,64,768]{2,1,0:T(8,128)(2,1)}), bf16[8,64,768]{2,1,0:T(8,128)(2,1)S(1)}, u32[]{:S(2)}, u32[]{:S(2)}) %all-to-all-start) | async-done | bytes 786464 | tf_op jit(solution)/shard_map/all_to_all | solution.py:105
  22.8 2.1 %collective-permute-start.1 = (bf16[64,256]{1,0:T(8,128)(2,1)S(1)}, bf16[64,256]{1,0:T(8,128)(2,1)S(1)}, u32[]{:S(2)}, u32[]{:S(2)}) collective-permute-start(bf16[64,256]{1,0:T(8,128)(2,1)S(1)} %convolution_convert_fusion), channel_id=1, source_target_pairs={{0,8},{8,0},{16,24},{24,16},{32,40},{40,32},{48,56},{56,48},{64,72... | collective-permute-start | bytes 98312 | tf_op jit(solution)/shard_map/ppermute | solution.py:16
  26.1 2.6 %collective-permute-start.2 = (bf16[64,256]{1,0:T(8,128)(2,1)S(1)}, bf16[64,256]{1,0:T(8,128)(2,1)S(1)}, u32[]{:S(2)}, u32[]{:S(2)}) collective-permute-start(bf16[64,256]{1,0:T(8,128)(2,1)S(1)} %add.30), channel_id=1, source_target_pairs={{0,16},{8,24},{16,0},{24,8},{32,48},{40,56},{48,32},{56,40},{64,80... | collective-permute-start | bytes 98312 | tf_op jit(solution)/shard_map/ppermute | solution.py:16
  28.7 3.2 %collective-permute-done.2 = bf16[64,256]{1,0:T(8,128)(2,1)S(1)} collective-permute-done((bf16[64,256]{1,0:T(8,128)(2,1)S(1)}, bf16[64,256]{1,0:T(8,128)(2,1)S(1)}, u32[]{:S(2)}, u32[]{:S(2)}) %collective-permute-start.2) | collective-permute-done | bytes 32800 | tf_op jit(solution)/shard_map/ppermute | solution.py:16
  31.9 2.0 %collective-permute-start.3 = (bf16[64,256]{1,0:T(8,128)(2,1)S(1)}, bf16[64,256]{1,0:T(8,128)(2,1)S(1)}, u32[]{:S(2)}, u32[]{:S(2)}) collective-permute-start(bf16[64,256]{1,0:T(8,128)(2,1)S(1)} %add.31), channel_id=1, source_target_pairs={{0,32},{8,40},{16,48},{24,56},{32,0},{40,8},{48,16},{56,24},{64,96... | collective-permute-start | bytes 98312 | tf_op jit(solution)/shard_map/ppermute | solution.py:16
  34.0 13.9 %collective-permute-start.7 = (bf16[8,64,256]{2,1,0:T(8,128)(2,1)S(1)}, bf16[8,64,256]{2,1,0:T(8,128)(2,1)}, u32[]{:S(2)}, u32[]{:S(2)}) collective-permute-start(bf16[8,64,256]{2,1,0:T(8,128)(2,1)S(1)} %pad_maximum_fusion.1), channel_id=1, source_target_pairs={{0,256},{8,264},{16,272},{24,280},{32,288},{40,296},{48,304},{56,3... | collective-permute-start | bytes 786440 | tf_op jit(solution)/shard_map/ppermute | solution.py:16
  47.9 3.4 %collective-permute-start.4 = (bf16[64,256]{1,0:T(8,128)(2,1)S(1)}, bf16[64,256]{1,0:T(8,128)(2,1)S(1)}, u32[]{:S(2)}, u32[]{:S(2)}) collective-permute-start(bf16[64,256]{1,0:T(8,128)(2,1)S(1)} %add.32), channel_id=1, source_target_pairs={{0,64},{8,72},{16,80},{24,88},{32,96},{40,104},{48,112},{56,120},{... | collective-permute-start | bytes 98312 | tf_op jit(solution)/shard_map/ppermute | solution.py:16
  51.3 20.7 %collective-permute-done.4 = bf16[64,256]{1,0:T(8,128)(2,1)S(1)} collective-permute-done((bf16[64,256]{1,0:T(8,128)(2,1)S(1)}, bf16[64,256]{1,0:T(8,128)(2,1)S(1)}, u32[]{:S(2)}, u32[]{:S(2)}) %collective-permute-start.4) | collective-permute-done | bytes 32800 | tf_op jit(solution)/shard_map/ppermute | solution.py:16
  72.0 1.9 %collective-permute-start.5 = (bf16[64,256]{1,0:T(8,128)(2,1)S(1)}, bf16[64,256]{1,0:T(8,128)(2,1)S(1)}, u32[]{:S(2)}, u32[]{:S(2)}) collective-permute-start(bf16[64,256]{1,0:T(8,128)(2,1)S(1)} %add.33), channel_id=1, source_target_pairs={{0,128},{8,136},{16,144},{24,152},{32,160},{40,168},{48,176},{56,1... | collective-permute-start | bytes 98312 | tf_op jit(solution)/shard_map/ppermute | solution.py:16
  74.1 7.6 %collective-permute-done.5 = bf16[64,256]{1,0:T(8,128)(2,1)S(1)} collective-permute-done((bf16[64,256]{1,0:T(8,128)(2,1)S(1)}, bf16[64,256]{1,0:T(8,128)(2,1)S(1)}, u32[]{:S(2)}, u32[]{:S(2)}) %collective-permute-start.5) | collective-permute-done | bytes 32800 | tf_op jit(solution)/shard_map/ppermute | solution.py:16
  81.7 1.9 %collective-permute-start.6 = (bf16[64,256]{1,0:T(8,128)(2,1)S(1)}, bf16[64,256]{1,0:T(8,128)(2,1)S(1)}, u32[]{:S(2)}, u32[]{:S(2)}) collective-permute-start(bf16[64,256]{1,0:T(8,128)(2,1)S(1)} %add.34), channel_id=1, source_target_pairs={{0,256},{8,264},{16,272},{24,280},{32,288},{40,296},{48,304},{56,3... | collective-permute-start | bytes 98312 | tf_op jit(solution)/shard_map/ppermute | solution.py:16
  83.7 3.8 %all-to-all-start.1 = ((bf16[8,64,256]{2,1,0:T(8,128)(2,1)}), bf16[8,64,256]{2,1,0:T(8,128)(2,1)S(1)}, u32[]{:S(2)}, u32[]{:S(2)}) async-start(bf16[8,64,256]{2,1,0:T(8,128)(2,1)} %collective-permute-done.7), calls=%async_computation.1 | async-start | bytes 524288 | tf_op jit(solution)/shard_map/all_to_all | solution.py:105
  87.6 2.6 %collective-permute-start.11 = (bf16[512,256]{1,0:T(8,128)(2,1)S(1)}, bf16[512,256]{1,0:T(8,128)(2,1)S(1)}, u32[]{:S(2)}, u32[]{:S(2)}) collective-permute-start(bf16[512,256]{1,0:T(8,128)(2,1)S(1)} %slice.13.refs_0_), channel_id=1, source_target_pairs={{0,16},{8,24},{16,0},{24,8},{32,48},{40,56},{48,32},{56,40},{64,80... | collective-permute-start | bytes 786440 | tf_op jit(solution)/shard_map/ppermute | solution.py:16
  90.2 1.9 %collective-permute-start.10 = (bf16[512,256]{1,0:T(8,128)(2,1)S(1)}, bf16[512,256]{1,0:T(8,128)(2,1)S(1)}, u32[]{:S(2)}, u32[]{:S(2)}) collective-permute-start(bf16[512,256]{1,0:T(8,128)(2,1)S(1)} %slice.13.refs_0_), channel_id=1, source_target_pairs={{0,8},{8,0},{16,24},{24,16},{32,40},{40,32},{48,56},{56,48},{64,72... | collective-permute-start | bytes 786440 | tf_op jit(solution)/shard_map/ppermute | solution.py:16
  92.1 4.0 %collective-permute-start.9 = (bf16[512,256]{1,0:T(8,128)(2,1)S(1)}, bf16[512,256]{1,0:T(8,128)(2,1)S(1)}, u32[]{:S(2)}, u32[]{:S(2)}) collective-permute-start(bf16[512,256]{1,0:T(8,128)(2,1)S(1)} %slice.13.refs_0_), channel_id=1, source_target_pairs={{0,64},{8,72},{16,80},{24,88},{32,96},{40,104},{48,112},{56,120},{... | collective-permute-start | bytes 786440 | tf_op jit(solution)/shard_map/ppermute | solution.py:16
  96.1 4.0 %collective-permute-start.8 = (bf16[512,256]{1,0:T(8,128)(2,1)S(1)}, bf16[512,256]{1,0:T(8,128)(2,1)S(1)}, u32[]{:S(2)}, u32[]{:S(2)}) collective-permute-start(bf16[512,256]{1,0:T(8,128)(2,1)S(1)} %slice.13.refs_0_), channel_id=1, source_target_pairs={{0,32},{8,40},{16,48},{24,56},{32,0},{40,8},{48,16},{56,24},{64,96... | collective-permute-start | bytes 786440 | tf_op jit(solution)/shard_map/ppermute | solution.py:16
  100.1 2.4 %collective-permute-start = (bf16[512,256]{1,0:T(8,128)(2,1)S(1)}, bf16[512,256]{1,0:T(8,128)(2,1)S(1)}, u32[]{:S(2)}, u32[]{:S(2)}) collective-permute-start(bf16[512,256]{1,0:T(8,128)(2,1)S(1)} %slice.13.refs_0_), channel_id=1, source_target_pairs={{0,128},{8,136},{16,144},{24,152},{32,160},{40,168},{48,176},{56,1... | collective-permute-start | bytes 786440 | tf_op jit(solution)/shard_map/ppermute | solution.py:16
  103.3 7.5 %shard_map.73 = (f32[4,512,128]{2,1,0:T(8,128)S(1)}, f32[4,512,2]{2,1,0:T(8,128)S(1)}) custom-call(f32[3,4]{1,0:T(4,128)S(1)} %pad_maximum_fusion.2.bias_ref, bf16[512,512]{1,0:T(8,128)(2,1)S(1)} %slice.12.q_ref, bf16[512,256]{1,0:T(8,128)(2,1)S(1)} %slice.13.refs_0_, bf16[512,256]{1,0:T(8,128)(2,1)S(1)} %collective-permute-done.10.refs_1_, ...), custom_call_target="tpu_custom_call" | custom-call | tf_op jit(solution)/shard_map/pallas_call | solution.py:85
  110.8 12.1 %collective-permute-done.8.refs_0_ = bf16[512,256]{1,0:T(8,128)(2,1)S(1)} collective-permute-done((bf16[512,256]{1,0:T(8,128)(2,1)S(1)}, bf16[512,256]{1,0:T(8,128)(2,1)S(1)}, u32[]{:S(2)}, u32[]{:S(2)}) %collective-permute-start.8) | collective-permute-done | bytes 262176 | tf_op jit(solution)/shard_map/ppermute | solution.py:16
  122.9 6.8 %shard_map.74 = (f32[4,512,128]{2,1,0:T(8,128)S(1)}, f32[4,512,2]{2,1,0:T(8,128)S(1)}) custom-call(f32[2,4]{1,0:T(2,128)S(1)} %pad_maximum_fusion.4.bias_ref, bf16[512,512]{1,0:T(8,128)(2,1)S(1)} %slice.12.q_ref, bf16[512,256]{1,0:T(8,128)(2,1)S(1)} %collective-permute-done.8.refs_0_, bf16[512,256]{1,0:T(8,128)(2,1)S(1)} %collective-permute-done.9.refs_1_, ...), custom_call_target="tpu_custom_call" | custom-call | tf_op jit(solution)/shard_map/pallas_call | solution.py:85
  129.8 5.3 %shard_map.75 = (f32[4,512,128]{2,1,0:T(8,128)S(1)}, f32[4,512,2]{2,1,0:T(8,128)S(1)}) custom-call(f32[1,4]{1,0:T(1,128)S(1)} %bitcast.49, bf16[512,512]{1,0:T(8,128)(2,1)S(1)} %slice.12.q_ref, bf16[512,256]{1,0:T(8,128)(2,1)S(1)} %bitcast.48, f32[4,512,128]{2,1,0:T(8,128)S(1)} %get-tuple-element.13.refs_1_, f32[4,512,2]{2,1,0:T(8,128)S(1)} %get-tuple-element.14.refs_2_), custom_call_target="tpu_custom_call" | custom-call | tf_op jit(solution)/shard_map/pallas_call | solution.py:85
  135.1 5.8 %shard_map.76 = bf16[512,512]{1,0:T(8,128)(2,1)S(1)} custom-call(f32[2,4]{1,0:T(2,128)S(1)} %pad_maximum_fusion.3.bias_ref, bf16[512,512]{1,0:T(8,128)(2,1)S(1)} %slice.12.q_ref, bf16[512,256]{1,0:T(8,128)(2,1)S(1)} %collective-permute-done.refs_0_, bf16[64,256]{1,0:T(8,128)(2,1)S(1)} %copy-done.1, f32[4,512,128]{2,1,0:T(8,128)S(1)} %get-tuple-element.15.refs_2_, ...), custom_call_target="tpu_custom_call" | custom-call | tf_op jit(solution)/shard_map/pallas_call | solution.py:85
  140.9 18.3 %all_to_all.29 = bf16[8,64,512]{2,1,0:T(8,128)(2,1)S(1)} all-to-all(bf16[8,64,512]{2,1,0:T(8,128)(2,1)S(1)} %bitcast.47), channel_id=1, replica_groups=mesh['seq'=64,'head'=8] {'head'}, dimensions={0} | all-to-all | bytes 1048576 | tf_op jit(solution)/shard_map/all_to_all | solution.py:134
  (44 shorter events, 5.5 us)
Async XLA Ops:
  0.0 1.1 copy-start
  0.0 1.1 copy-start.2
  2.2 20.4 %copy-start.6 = (s32[64]{0:T(128)S(1)}, s32[64]{0:T(128)}, u32[]{:S(2)}) copy-start(s32[64]{0:T(128)} %param.13) | copy-start | bytes 772
  2.2 49.1 %copy-start.5 = (s32[1,6]{1,0:T(1,128)S(1)}, s32[1,6]{1,0:T(1,128)}, u32[]{:S(2)}) copy-start(s32[1,6]{1,0:T(1,128)} %param.12) | copy-start | bytes 76
  2.2 20.4 %all-to-all-start = ((bf16[8,64,768]{2,1,0:T(8,128)(2,1)}), bf16[8,64,768]{2,1,0:T(8,128)(2,1)S(1)}, u32[]{:S(2)}, u32[]{:S(2)}) async-start(bf16[8,64,768]{2,1,0:T(8,128)(2,1)} %pad_maximum_fusion), calls=%async_computation | async-start | bytes 1572864 | tf_op jit(solution)/shard_map/all_to_all | solution.py:105
  9.3 64.7 %copy-start.3 = (f32[4,6]{1,0:T(4,128)S(1)}, f32[4,6]{1,0:T(4,128)}, u32[]{:S(2)}) copy-start(f32[4,6]{1,0:T(4,128)} %param.10) | copy-start | bytes 292
  22.8 79.7 %copy-start.4 = (f32[4]{0:T(128)S(1)}, f32[4]{0:T(128)}, u32[]{:S(2)}) copy-start(f32[4]{0:T(128)} %param.11) | copy-start | bytes 52
  22.8 3.2 %collective-permute-start.1 = (bf16[64,256]{1,0:T(8,128)(2,1)S(1)}, bf16[64,256]{1,0:T(8,128)(2,1)S(1)}, u32[]{:S(2)}, u32[]{:S(2)}) collective-permute-start(bf16[64,256]{1,0:T(8,128)(2,1)S(1)} %convolution_convert_fusion), channel_id=1, source_target_pairs={{0,8},{8,0},{16,24},{24,16},{32,40},{40,32},{48,56},{56,48},{64,72... | collective-permute-start | bytes 98312 | tf_op jit(solution)/shard_map/ppermute | solution.py:16
  26.1 5.8 %collective-permute-start.2 = (bf16[64,256]{1,0:T(8,128)(2,1)S(1)}, bf16[64,256]{1,0:T(8,128)(2,1)S(1)}, u32[]{:S(2)}, u32[]{:S(2)}) collective-permute-start(bf16[64,256]{1,0:T(8,128)(2,1)S(1)} %add.30), channel_id=1, source_target_pairs={{0,16},{8,24},{16,0},{24,8},{32,48},{40,56},{48,32},{56,40},{64,80... | collective-permute-start | bytes 98312 | tf_op jit(solution)/shard_map/ppermute | solution.py:16
  31.9 16.0 %collective-permute-start.3 = (bf16[64,256]{1,0:T(8,128)(2,1)S(1)}, bf16[64,256]{1,0:T(8,128)(2,1)S(1)}, u32[]{:S(2)}, u32[]{:S(2)}) collective-permute-start(bf16[64,256]{1,0:T(8,128)(2,1)S(1)} %add.31), channel_id=1, source_target_pairs={{0,32},{8,40},{16,48},{24,56},{32,0},{40,8},{48,16},{56,24},{64,96... | collective-permute-start | bytes 98312 | tf_op jit(solution)/shard_map/ppermute | solution.py:16
  34.0 49.7 %collective-permute-start.7 = (bf16[8,64,256]{2,1,0:T(8,128)(2,1)S(1)}, bf16[8,64,256]{2,1,0:T(8,128)(2,1)}, u32[]{:S(2)}, u32[]{:S(2)}) collective-permute-start(bf16[8,64,256]{2,1,0:T(8,128)(2,1)S(1)} %pad_maximum_fusion.1), channel_id=1, source_target_pairs={{0,256},{8,264},{16,272},{24,280},{32,288},{40,296},{48,304},{56,3... | collective-permute-start | bytes 786440 | tf_op jit(solution)/shard_map/ppermute | solution.py:16
  47.9 24.1 %collective-permute-start.4 = (bf16[64,256]{1,0:T(8,128)(2,1)S(1)}, bf16[64,256]{1,0:T(8,128)(2,1)S(1)}, u32[]{:S(2)}, u32[]{:S(2)}) collective-permute-start(bf16[64,256]{1,0:T(8,128)(2,1)S(1)} %add.32), channel_id=1, source_target_pairs={{0,64},{8,72},{16,80},{24,88},{32,96},{40,104},{48,112},{56,120},{... | collective-permute-start | bytes 98312 | tf_op jit(solution)/shard_map/ppermute | solution.py:16
  72.0 9.7 %collective-permute-start.5 = (bf16[64,256]{1,0:T(8,128)(2,1)S(1)}, bf16[64,256]{1,0:T(8,128)(2,1)S(1)}, u32[]{:S(2)}, u32[]{:S(2)}) collective-permute-start(bf16[64,256]{1,0:T(8,128)(2,1)S(1)} %add.33), channel_id=1, source_target_pairs={{0,128},{8,136},{16,144},{24,152},{32,160},{40,168},{48,176},{56,1... | collective-permute-start | bytes 98312 | tf_op jit(solution)/shard_map/ppermute | solution.py:16
  81.7 18.4 %collective-permute-start.6 = (bf16[64,256]{1,0:T(8,128)(2,1)S(1)}, bf16[64,256]{1,0:T(8,128)(2,1)S(1)}, u32[]{:S(2)}, u32[]{:S(2)}) collective-permute-start(bf16[64,256]{1,0:T(8,128)(2,1)S(1)} %add.34), channel_id=1, source_target_pairs={{0,256},{8,264},{16,272},{24,280},{32,288},{40,296},{48,304},{56,3... | collective-permute-start | bytes 98312 | tf_op jit(solution)/shard_map/ppermute | solution.py:16
  83.7 46.0 %all-to-all-start.1 = ((bf16[8,64,256]{2,1,0:T(8,128)(2,1)}), bf16[8,64,256]{2,1,0:T(8,128)(2,1)S(1)}, u32[]{:S(2)}, u32[]{:S(2)}) async-start(bf16[8,64,256]{2,1,0:T(8,128)(2,1)} %collective-permute-done.7), calls=%async_computation.1 | async-start | bytes 524288 | tf_op jit(solution)/shard_map/all_to_all | solution.py:105
  87.6 15.7 %collective-permute-start.11 = (bf16[512,256]{1,0:T(8,128)(2,1)S(1)}, bf16[512,256]{1,0:T(8,128)(2,1)S(1)}, u32[]{:S(2)}, u32[]{:S(2)}) collective-permute-start(bf16[512,256]{1,0:T(8,128)(2,1)S(1)} %slice.13.refs_0_), channel_id=1, source_target_pairs={{0,16},{8,24},{16,0},{24,8},{32,48},{40,56},{48,32},{56,40},{64,80... | collective-permute-start | bytes 786440 | tf_op jit(solution)/shard_map/ppermute | solution.py:16
  90.2 13.1 %collective-permute-start.10 = (bf16[512,256]{1,0:T(8,128)(2,1)S(1)}, bf16[512,256]{1,0:T(8,128)(2,1)S(1)}, u32[]{:S(2)}, u32[]{:S(2)}) collective-permute-start(bf16[512,256]{1,0:T(8,128)(2,1)S(1)} %slice.13.refs_0_), channel_id=1, source_target_pairs={{0,8},{8,0},{16,24},{24,16},{32,40},{40,32},{48,56},{56,48},{64,72... | collective-permute-start | bytes 786440 | tf_op jit(solution)/shard_map/ppermute | solution.py:16
  92.1 18.7 %collective-permute-start.9 = (bf16[512,256]{1,0:T(8,128)(2,1)S(1)}, bf16[512,256]{1,0:T(8,128)(2,1)S(1)}, u32[]{:S(2)}, u32[]{:S(2)}) collective-permute-start(bf16[512,256]{1,0:T(8,128)(2,1)S(1)} %slice.13.refs_0_), channel_id=1, source_target_pairs={{0,64},{8,72},{16,80},{24,88},{32,96},{40,104},{48,112},{56,120},{... | collective-permute-start | bytes 786440 | tf_op jit(solution)/shard_map/ppermute | solution.py:16
  96.1 26.8 %collective-permute-start.8 = (bf16[512,256]{1,0:T(8,128)(2,1)S(1)}, bf16[512,256]{1,0:T(8,128)(2,1)S(1)}, u32[]{:S(2)}, u32[]{:S(2)}) collective-permute-start(bf16[512,256]{1,0:T(8,128)(2,1)S(1)} %slice.13.refs_0_), channel_id=1, source_target_pairs={{0,32},{8,40},{16,48},{24,56},{32,0},{40,8},{48,16},{56,24},{64,96... | collective-permute-start | bytes 786440 | tf_op jit(solution)/shard_map/ppermute | solution.py:16
  100.1 35.0 %collective-permute-start = (bf16[512,256]{1,0:T(8,128)(2,1)S(1)}, bf16[512,256]{1,0:T(8,128)(2,1)S(1)}, u32[]{:S(2)}, u32[]{:S(2)}) collective-permute-start(bf16[512,256]{1,0:T(8,128)(2,1)S(1)} %slice.13.refs_0_), channel_id=1, source_target_pairs={{0,128},{8,136},{16,144},{24,152},{32,160},{40,168},{48,176},{56,1... | collective-permute-start | bytes 786440 | tf_op jit(solution)/shard_map/ppermute | solution.py:16
  129.7 5.4 %copy-start.1 = (bf16[64,256]{1,0:T(8,128)(2,1)S(1)}, bf16[64,256]{1,0:T(8,128)(2,1)}, u32[]{:S(2)}) copy-start(bf16[64,256]{1,0:T(8,128)(2,1)} %add.35.refs_1_) | copy-start | bytes 98308

commit v2 on v1

v2 whole, which is shorter than its diff:
```python
import functools
import math

import jax
import jax.numpy as jnp
from jax import lax
from jax.experimental import pallas as pl
from jax.experimental.pallas import tpu as pltpu
from jax.sharding import PartitionSpec as P

HD = 128
LOG2E = math.log2(math.e)


def swap(value, bit):
    return lax.ppermute(value, "seq", [(i, i ^ bit) for i in range(lax.axis_size("seq"))])


def attend_kernel(count, first, final, bias_ref, q_ref, *refs):
    k_refs, v_refs, refs = refs[: 2 * count : 2], refs[1 : 2 * count : 2], refs[2 * count :]
    if not first:
        acc_in, stat_in, refs = refs[0], refs[1], refs[2:]
    scale = HD**-0.5 * LOG2E
    rows, heads = q_ref.shape[0], q_ref.shape[1] // HD
    tile = 256
    for head in range(heads):
        for start in range(0, rows, tile):
            part, cols = pl.ds(start, tile), pl.ds(head * HD, HD)
            query = q_ref[part, cols]
            scores, top = [], None
            for j in range(count):
                s = lax.dot_general(
                    query, k_refs[j][...], (((1,), (1,)), ((), ())), preferred_element_type=jnp.float32
                )
                bias = bias_ref[j, head] * LOG2E
                most = jnp.max(s, axis=-1, keepdims=True) * scale + bias
                top = most if top is None else jnp.maximum(top, most)
                scores.append((s, bias))
            if first:
                top = jnp.broadcast_to(top, (tile, HD))
            else:
                old_top = jnp.broadcast_to(stat_in[part, head : head + 1], (tile, HD))
                top = jnp.maximum(old_top, top)
            total = None
            for j in range(count):
                s, bias = scores[j]
                weights = jnp.exp2(s * scale - (top[:, :1] - bias)).astype(jnp.bfloat16)
                value = v_refs[j][...]
                widened = jnp.concatenate([value, jnp.ones_like(value)], axis=1)
                update = jnp.dot(weights, widened, preferred_element_type=jnp.float32)
                total = update if total is None else total + update
            acc, summed = total[:, :HD], total[:, HD:]
            if not first:
                rescale = jnp.exp2(old_top - top)
                acc = acc + acc_in[part, cols] * rescale
                old_sum = stat_in[part, heads + head : heads + head + 1]
                summed = summed + jnp.broadcast_to(old_sum, (tile, HD)) * rescale
            if final:
                refs[0][part, cols] = (acc / summed).astype(jnp.bfloat16)
            else:
                refs[0][part, cols] = acc
                refs[1][part, head : head + 1] = top[:, :1]
                refs[1][part, heads + head : heads + head + 1] = summed[:, :1]


def attend(state, queries, blocks, biases, final=False):
    rows, heads = queries.shape[0], biases.shape[1]
    width, count, first = heads * HD, len(blocks), state is None
    steps = 2

    def by_rows(columns):
        return pl.BlockSpec((rows // steps, columns), lambda i: (i, 0))

    def columns_at(size, place):
        return pl.BlockSpec((size, HD), lambda i: (0, place))

    state_specs = (by_rows(width), by_rows(2 * heads))
    in_specs = [pl.BlockSpec(memory_space=pltpu.SMEM), by_rows(width)]
    args = [biases, queries]
    for size, key_array, key_place, value_array, value_place in blocks:
        in_specs += [columns_at(size, key_place), columns_at(size, value_place)]
        args += [key_array, value_array]
    if not first:
        in_specs += state_specs
        args += state
    if final:
        out_shape, out_specs = jax.ShapeDtypeStruct((rows, width), jnp.bfloat16), by_rows(width)
    else:
        out_shape = tuple(jax.ShapeDtypeStruct((rows, n), jnp.float32) for n in (width, 2 * heads))
        out_specs = state_specs
    return pl.pallas_call(
        functools.partial(attend_kernel, count, first, final),
        grid=(steps,),
        in_specs=in_specs,
        out_specs=out_specs,
        out_shape=out_shape,
        compiler_params=pltpu.CompilerParams(vmem_limit_bytes=24 * 1024 * 1024),
    )(*args)


def on_device(queries, keys, values, level_bias, anchor_bias, partners, anchor_positions):
    tokens = queries.shape[0]
    shards = lax.axis_size("head")
    blocks = lax.axis_size("seq")
    block_index = lax.axis_index("seq")
    bits = blocks.bit_length() - 1
    after = lax.optimization_barrier
    places = queries.shape[1] // shards // HD
    rows = shards * tokens

    def by_head(array):
        return array.reshape(tokens, shards, -1).transpose(1, 0, 2)

    def to_heads(array):
        gathered = lax.all_to_all(array, "head", split_axis=0, concat_axis=0, tiled=True)
        return gathered.reshape(rows, -1)

    def from_four(array, offsets):
        groups = [
            [base ^ offset for offset in offsets]
            for base in range(blocks)
            if base == min(base ^ offset for offset in offsets)
        ]
        copies = jnp.broadcast_to(array[None], (4, *array.shape))
        return lax.all_to_all(copies, "seq", split_axis=0, concat_axis=0, axis_index_groups=groups)

    chosen = [
        (partners[0] == jnp.bitwise_xor(block_index, 1 << bit)).astype(jnp.float32) for bit in range(bits)
    ]
    bias = jnp.concatenate(
        [jnp.zeros_like(anchor_bias)[None], jnp.stack(chosen) @ level_bias.T, anchor_bias[None]], axis=0
    )

    kv_shard = jnp.concatenate([by_head(keys), by_head(values)], axis=2)
    shard5, shard4 = swap(kv_shard, 32), swap(kv_shard, 16)
    qkv = to_heads(jnp.concatenate([by_head(queries), kv_shard], axis=2))
    kv = qkv[:, places * HD :]

    token_index = block_index * rows + jnp.arange(rows, dtype=jnp.int32)
    selector = (anchor_positions[:, None] == token_index[None, :]).astype(jnp.bfloat16)
    held = jnp.dot(selector, kv, preferred_element_type=jnp.float32).astype(jnp.bfloat16)
    near, level1 = swap(kv, 1), swap(kv, 2)
    plane = jnp.sum(from_four(held, (0, 1, 2, 3)), axis=0)
    state = attend(
        None,
        qkv,
        [(rows, qkv, places, qkv, places + 1), (rows, near, 0, near, 1), (rows, level1, 0, level1, 1)],
        bias[0:3],
    )
    carried = jnp.concatenate([kv, plane], axis=0)
    level3, level2, diagonal = swap(carried, 8), swap(carried, 4), swap(carried[rows:], 12)
    shard4, shard5, state, diagonal = after((shard4, shard5, state, diagonal))
    far = to_heads(jnp.concatenate([shard4, shard5], axis=2))
    mine = plane + level2[rows:] + level3[rows:] + diagonal
    anchors = mine + swap(mine, 16) + swap(mine, 32) + swap(mine, 48)
    count = anchors.shape[0]
    result = attend(
        state,
        qkv,
        [
            (rows, level2, 0, level2, 1),
            (rows, level3, 0, level3, 1),
            (rows, far, 0, far, 1),
            (rows, far, 2, far, 3),
            (count, anchors, 0, anchors, 1),
        ],
        bias[3:8],
        final=True,
    )
    return lax.all_to_all(result, "head", split_axis=0, concat_axis=1, tiled=True)


def solution(mesh):
    in_specs = (
        P(("seq", "head"), None),
        P(("seq", "head"), None),
        P(("seq", "head"), None),
        P("head", None),
        P("head"),
        P("seq", None),
        P(),
    )
    out_specs = P(("seq", "head"), None)
    return jax.shard_map(
        on_device, mesh=mesh, in_specs=in_specs, out_specs=out_specs, check_vma=False
    )
```

time: 161 us -> 139 us (0.86)
  waiting for transfers between devices: 58.1 us -> 26.3 us
  starting transfers between devices: 53.6 us -> 72.5 us
  Pallas kernels: 25.5 us -> 14.9 us
  other arithmetic: 1.98 us -> 4.39 us
    ppermute x12 -> x10, waiting for transfers between devices: 44.8 us -> 25.6 us  [swap(): lax.ppermute(value, 'seq', [(i, i ^ bit) for i in range(lax.axis_size('se...]
    all_to_all x2, waiting for transfers between devices: 13.3 us -> 0.01 us  [to_heads(): lax.all_to_all(array, 'head', split_axis=0, concat_axis=0, tiled=True)]
    ppermute x12 -> x10, starting transfers between devices: 42.7 us -> 55.2 us  [swap(): lax.ppermute(value, 'seq', [(i, i ^ bit) for i in range(lax.axis_size('se...]
    pallas_call x4 -> x2, Pallas kernels: 25.5 us -> 14.9 us  [attend(): pl.pallas_call(functools.partial(attend_kernel, count, first, final), gri...]
    all_to_all x0 -> x1, starting transfers between devices: none -> 3.32 us  [from_four(): lax.all_to_all(copies, 'seq', split_axis=0, concat_axis=0, axis_index_gro...]
    all_to_all x2, starting transfers between devices: 10.9 us -> 14 us  [to_heads(): lax.all_to_all(array, 'head', split_axis=0, concat_axis=0, tiled=True)]
    concatenate x0 -> x3, other arithmetic: none -> 2.62 us  [the longest x1 1.87 us: on_device(): far = to_heads(jnp.concatenate([shard4, shard5], axis=2))]
  transfers between devices with their start and end apart: 14 -> 13, of which waited for: 6 -> 5; matrix products, arithmetic and copies ran while one was open for 1% -> 3% of each run, Pallas kernels for 12% -> 4%
where the time goes in v2:
time: 139 us; the launch traced here: 138 us
  starting transfers between devices  72.5 us (52%)
  waiting for transfers between devices  26.3 us (19%)
  blocking collectives  16.8 us (12%)
  Pallas kernels  14.9 us (11%)
  other arithmetic  4.39 us (3%)
  local copies, waits for them, and re-layouts  2.77 us (2%)
    ppermute x10, starting transfers between devices, swap(): lax.ppermute(value, 'seq', [(i, i ^ bit) for i in range(lax.axis_size('se...  55.2 us
    ppermute x10, waiting for transfers between devices, swap(): lax.ppermute(value, 'seq', [(i, i ^ bit) for i in range(lax.axis_size('se...  25.6 us
    all_to_all x1, blocking collectives, on_device(): lax.all_to_all(result, 'head', split_axis=0, concat_axis=1, tiled=True)  16.8 us
    pallas_call x2, Pallas kernels, attend(): pl.pallas_call(functools.partial(attend_kernel, count, first, final), gri...  14.9 us
    all_to_all x2, starting transfers between devices, to_heads(): lax.all_to_all(array, 'head', split_axis=0, concat_axis=0, tiled=True)  14 us
    all_to_all x1, starting transfers between devices, from_four(): lax.all_to_all(copies, 'seq', split_axis=0, concat_axis=0, axis_index_gro...  3.32 us
  transfers between devices with their start and end apart: 13, of which 5 were waited for; matrix products, arithmetic and copies ran while one was open for 3% of the time, Pallas kernels for 4%

profile of v2, /device:TPU:96, one launch (start us, length us, event | category | flops | bytes accessed | tf_op | source)
XLA Modules:
  0.0 138.3 jit_solution(3011803433346657050)
XLA Ops:
  0.0 1.1 copy.28
  1.2 1.0 pad_maximum_fusion
  2.2 7.1 %all-to-all-start = ((bf16[8,64,768]{2,1,0:T(8,128)(2,1)}), bf16[8,64,768]{2,1,0:T(8,128)(2,1)S(1)}, u32[]{:S(2)}, u32[]{:S(2)}) async-start(bf16[8,64,768]{2,1,0:T(8,128)(2,1)} %pad_maximum_fusion), calls=%async_computation | async-start | bytes 1572864 | tf_op jit(solution)/shard_map/all_to_all | solution.py:115
  10.0 9.1 %collective-permute-start.2 = (bf16[8,64,256]{2,1,0:T(8,128)(2,1)}, bf16[8,64,256]{2,1,0:T(8,128)(2,1)}, u32[]{:S(2)}, u32[]{:S(2)}) collective-permute-start(bf16[8,64,256]{2,1,0:T(8,128)(2,1)} %pad_maximum_fusion.3), channel_id=1, source_target_pairs={{0,128},{8,136},{16,144},{24,152},{32,160},{40,168},{48,176},{56,1... | collective-permute-start | bytes 786440 | tf_op jit(solution)/shard_map/ppermute | solution.py:16
  19.1 8.2 %collective-permute-start.3 = (bf16[8,64,256]{2,1,0:T(8,128)(2,1)}, bf16[8,64,256]{2,1,0:T(8,128)(2,1)}, u32[]{:S(2)}, u32[]{:S(2)}) collective-permute-start(bf16[8,64,256]{2,1,0:T(8,128)(2,1)} %pad_maximum_fusion.3), channel_id=1, source_target_pairs={{0,256},{8,264},{16,272},{24,280},{32,288},{40,296},{48,304},{56,3... | collective-permute-start | bytes 786440 | tf_op jit(solution)/shard_map/ppermute | solution.py:16
  27.4 1.9 %collective-permute-start.4 = (bf16[512,256]{1,0:T(8,128)(2,1)S(1)}, bf16[512,256]{1,0:T(8,128)(2,1)S(1)}, u32[]{:S(2)}, u32[]{:S(2)}) collective-permute-start(bf16[512,256]{1,0:T(8,128)(2,1)S(1)} %slice.22), channel_id=1, source_target_pairs={{0,8},{8,0},{16,24},{24,16},{32,40},{40,32},{48,56},{56,48},{64,72... | collective-permute-start | bytes 786440 | tf_op jit(solution)/shard_map/ppermute | solution.py:16
  30.2 3.3 %all-to-all-start.1 = ((bf16[4,64,256]{2,1,0:T(8,128)(2,1)}), bf16[4,64,256]{2,1,0:T(8,128)(2,1)S(1)}, u32[]{:S(2)}, u32[]{:S(2)}) async-start(bf16[4,64,256]{2,1,0:T(8,128)(2,1)} %broadcast_in_dim.5), calls=%async_computation.1 | async-start | bytes 262144 | tf_op jit(solution)/shard_map/all_to_all | solution.py:125
  33.6 3.9 %collective-permute-start.5 = (bf16[512,256]{1,0:T(8,128)(2,1)S(1)}, bf16[512,256]{1,0:T(8,128)(2,1)S(1)}, u32[]{:S(2)}, u32[]{:S(2)}) collective-permute-start(bf16[512,256]{1,0:T(8,128)(2,1)S(1)} %slice.22), channel_id=1, source_target_pairs={{0,16},{8,24},{16,0},{24,8},{32,48},{40,56},{48,32},{56,40},{64,80... | collective-permute-start | bytes 786440 | tf_op jit(solution)/shard_map/ppermute | solution.py:16
  38.9 2.9 %collective-permute-start = (bf16[576,256]{1,0:T(8,128)(2,1)}, bf16[576,256]{1,0:T(8,128)(2,1)S(1)}, u32[]{:S(2)}, u32[]{:S(2)}) collective-permute-start(bf16[576,256]{1,0:T(8,128)(2,1)} %pad_maximum_fusion.2), channel_id=1, source_target_pairs={{0,32},{8,40},{16,48},{24,56},{32,0},{40,8},{48,16},{56,24},{64,96... | collective-permute-start | bytes 884744 | tf_op jit(solution)/shard_map/ppermute | solution.py:16
  41.8 3.4 %collective-permute-start.1 = (bf16[576,256]{1,0:T(8,128)(2,1)}, bf16[576,256]{1,0:T(8,128)(2,1)S(1)}, u32[]{:S(2)}, u32[]{:S(2)}) collective-permute-start(bf16[576,256]{1,0:T(8,128)(2,1)} %pad_maximum_fusion.2), channel_id=1, source_target_pairs={{0,64},{8,72},{16,80},{24,88},{32,96},{40,104},{48,112},{56,120},{... | collective-permute-start | bytes 884744 | tf_op jit(solution)/shard_map/ppermute | solution.py:16
  45.3 3.8 %collective-permute-start.6 = (bf16[64,256]{1,0:T(8,128)(2,1)S(1)}, bf16[64,256]{1,0:T(8,128)(2,1)S(1)}, u32[]{:S(2)}, u32[]{:S(2)}) collective-permute-start(bf16[64,256]{1,0:T(8,128)(2,1)S(1)} %reduce_sum.12), channel_id=1, source_target_pairs={{0,96},{8,104},{16,112},{24,120},{32,64},{40,72},{48,80},{56,88},{... | collective-permute-start | bytes 98312 | tf_op jit(solution)/shard_map/ppermute | solution.py:16
  49.2 5.9 %shard_map.73 = (f32[512,512]{1,0:T(8,128)S(1)}, f32[512,8]{1,0:T(8,128)S(1)}) custom-call(f32[3,4]{1,0:T(4,128)S(1)} %pad_slice_fusion.bias_ref, bf16[512,768]{1,0:T(8,128)(2,1)S(1)} %bitcast.32, bf16[512,768]{1,0:T(8,128)(2,1)S(1)} %bitcast.33, bf16[512,768]{1,0:T(8,128)(2,1)S(1)} %bitcast.34, bf16[512,256]{1,0:T(8,128)(2,1)S(1)} %collective-permute-done.4.refs_2_.refs_3_, ...), custom_call_target="tpu_custom_call" | custom-call | tf_op jit(solution)/shard_map/pallas_call | solution.py:91
  55.1 3.1 %collective-permute-done.2 = bf16[8,64,256]{2,1,0:T(8,128)(2,1)} collective-permute-done((bf16[8,64,256]{2,1,0:T(8,128)(2,1)}, bf16[8,64,256]{2,1,0:T(8,128)(2,1)}, u32[]{:S(2)}, u32[]{:S(2)}) %collective-permute-start.2) | collective-permute-done | bytes 262176 | tf_op jit(solution)/shard_map/ppermute | solution.py:16
  58.1 14.8 %collective-permute-done.6 = bf16[64,256]{1,0:T(8,128)(2,1)S(1)} collective-permute-done((bf16[64,256]{1,0:T(8,128)(2,1)S(1)}, bf16[64,256]{1,0:T(8,128)(2,1)S(1)}, u32[]{:S(2)}, u32[]{:S(2)}) %collective-permute-start.6) | collective-permute-done | bytes 32800 | tf_op jit(solution)/shard_map/ppermute | solution.py:16
  73.0 1.9 %pad_maximum_fusion.1 = bf16[8,64,512]{2,1,0:T(8,128)(2,1)} fusion(bf16[8,64,256]{2,1,0:T(8,128)(2,1)} %collective-permute-done.3, bf16[8,64,256]{2,1,0:T(8,128)(2,1)} %collective-permute-done.2), kind=kLoop, calls=%fused_computation.3 | loop fusion | flops 1048576 | bytes 1048576 | tf_op jit(solution)/shard_map/concatenate | solution.py:153
  74.8 6.9 %all-to-all-start.2 = ((bf16[8,64,512]{2,1,0:T(8,128)(2,1)}), bf16[8,64,512]{2,1,0:T(8,128)(2,1)S(1)}, u32[]{:S(2)}, u32[]{:S(2)}) async-start(bf16[8,64,512]{2,1,0:T(8,128)(2,1)} %pad_maximum_fusion.1), calls=%async_computation.2 | async-start | bytes 1048576 | tf_op jit(solution)/shard_map/all_to_all | solution.py:115
  81.8 11.2 %collective-permute-start.7 = (bf16[64,256]{1,0:T(8,128)(2,1)S(1)}, bf16[64,256]{1,0:T(8,128)(2,1)S(1)}, u32[]{:S(2)}, u32[]{:S(2)}) collective-permute-start(bf16[64,256]{1,0:T(8,128)(2,1)S(1)} %fusion.3), channel_id=1, source_target_pairs={{0,128},{8,136},{16,144},{24,152},{32,160},{40,168},{48,176},{56,1... | collective-permute-start | bytes 98312 | tf_op jit(solution)/shard_map/ppermute | solution.py:16
  93.0 8.9 %collective-permute-start.8 = (bf16[64,256]{1,0:T(8,128)(2,1)S(1)}, bf16[64,256]{1,0:T(8,128)(2,1)S(1)}, u32[]{:S(2)}, u32[]{:S(2)}) collective-permute-start(bf16[64,256]{1,0:T(8,128)(2,1)S(1)} %fusion.3), channel_id=1, source_target_pairs={{0,256},{8,264},{16,272},{24,280},{32,288},{40,296},{48,304},{56,3... | collective-permute-start | bytes 98312 | tf_op jit(solution)/shard_map/ppermute | solution.py:16
  101.9 1.9 %collective-permute-start.9 = (bf16[64,256]{1,0:T(8,128)(2,1)S(1)}, bf16[64,256]{1,0:T(8,128)(2,1)S(1)}, u32[]{:S(2)}, u32[]{:S(2)}) collective-permute-start(bf16[64,256]{1,0:T(8,128)(2,1)S(1)} %fusion.3), channel_id=1, source_target_pairs={{0,384},{8,392},{16,400},{24,408},{32,416},{40,424},{48,432},{56,4... | collective-permute-start | bytes 98312 | tf_op jit(solution)/shard_map/ppermute | solution.py:16
  103.9 3.6 %collective-permute-done.8 = bf16[64,256]{1,0:T(8,128)(2,1)S(1)} collective-permute-done((bf16[64,256]{1,0:T(8,128)(2,1)S(1)}, bf16[64,256]{1,0:T(8,128)(2,1)S(1)}, u32[]{:S(2)}, u32[]{:S(2)}) %collective-permute-start.8) | collective-permute-done | bytes 32800 | tf_op jit(solution)/shard_map/ppermute | solution.py:16
  107.5 4.1 %collective-permute-done.9 = bf16[64,256]{1,0:T(8,128)(2,1)S(1)} collective-permute-done((bf16[64,256]{1,0:T(8,128)(2,1)S(1)}, bf16[64,256]{1,0:T(8,128)(2,1)S(1)}, u32[]{:S(2)}, u32[]{:S(2)}) %collective-permute-start.9) | collective-permute-done | bytes 32800 | tf_op jit(solution)/shard_map/ppermute | solution.py:16
  111.7 9.0 %shard_map.74 = bf16[512,512]{1,0:T(8,128)(2,1)S(1)} custom-call(f32[5,4]{1,0:T(8,128)S(1)} %slice.17.bias_ref, bf16[512,768]{1,0:T(8,128)(2,1)S(1)} %bitcast.35, bf16[576,256]{1,0:T(8,128)(2,1)S(1)} %collective-permute-done.refs_0_.refs_1_, bf16[576,256]{1,0:T(8,128)(2,1)S(1)} %collective-permute-done.refs_0_.refs_1_, ...), custom_call_target="tpu_custom_call" | custom-call | tf_op jit(solution)/shard_map/pallas_call | solution.py:91
  120.7 16.8 %all_to_all.34 = bf16[8,64,512]{2,1,0:T(8,128)(2,1)S(1)} all-to-all(bf16[8,64,512]{2,1,0:T(8,128)(2,1)S(1)} %bitcast.40), channel_id=1, replica_groups=mesh['seq'=64,'head'=8] {'head'}, dimensions={0} | all-to-all | bytes 1048576 | tf_op jit(solution)/shard_map/all_to_all | solution.py:170
  137.5 0.8 copy.24
  (37 shorter events, 3.4 us)
Async XLA Ops:
  0.0 1.1 copy-start
  0.0 1.1 copy-start.1
  2.2 27.1 %copy-start.5 = (s32[64]{0:T(128)S(1)}, s32[64]{0:T(128)}, u32[]{:S(2)}) copy-start(s32[64]{0:T(128)} %param.13) | copy-start | bytes 772
  2.2 25.2 %all-to-all-start = ((bf16[8,64,768]{2,1,0:T(8,128)(2,1)}), bf16[8,64,768]{2,1,0:T(8,128)(2,1)S(1)}, u32[]{:S(2)}, u32[]{:S(2)}) async-start(bf16[8,64,768]{2,1,0:T(8,128)(2,1)} %pad_maximum_fusion), calls=%async_computation | async-start | bytes 1572864 | tf_op jit(solution)/shard_map/all_to_all | solution.py:115
  9.3 24.3 %copy-start.4 = (s32[1,6]{1,0:T(1,128)S(1)}, s32[1,6]{1,0:T(1,128)}, u32[]{:S(2)}) copy-start(s32[1,6]{1,0:T(1,128)} %param.12) | copy-start | bytes 76
  10.0 48.1 %collective-permute-start.2 = (bf16[8,64,256]{2,1,0:T(8,128)(2,1)}, bf16[8,64,256]{2,1,0:T(8,128)(2,1)}, u32[]{:S(2)}, u32[]{:S(2)}) collective-permute-start(bf16[8,64,256]{2,1,0:T(8,128)(2,1)} %pad_maximum_fusion.3), channel_id=1, source_target_pairs={{0,128},{8,136},{16,144},{24,152},{32,160},{40,168},{48,176},{56,1... | collective-permute-start | bytes 786440 | tf_op jit(solution)/shard_map/ppermute | solution.py:16
  19.1 39.1 %collective-permute-start.3 = (bf16[8,64,256]{2,1,0:T(8,128)(2,1)}, bf16[8,64,256]{2,1,0:T(8,128)(2,1)}, u32[]{:S(2)}, u32[]{:S(2)}) collective-permute-start(bf16[8,64,256]{2,1,0:T(8,128)(2,1)} %pad_maximum_fusion.3), channel_id=1, source_target_pairs={{0,256},{8,264},{16,272},{24,280},{32,288},{40,296},{48,304},{56,3... | collective-permute-start | bytes 786440 | tf_op jit(solution)/shard_map/ppermute | solution.py:16
  27.3 17.9 %copy-start.2 = (f32[4,6]{1,0:T(4,128)S(1)}, f32[4,6]{1,0:T(4,128)}, u32[]{:S(2)}) copy-start(f32[4,6]{1,0:T(4,128)} %param.10) | copy-start | bytes 292
  27.4 14.4 %collective-permute-start.4 = (bf16[512,256]{1,0:T(8,128)(2,1)S(1)}, bf16[512,256]{1,0:T(8,128)(2,1)S(1)}, u32[]{:S(2)}, u32[]{:S(2)}) collective-permute-start(bf16[512,256]{1,0:T(8,128)(2,1)S(1)} %slice.22), channel_id=1, source_target_pairs={{0,8},{8,0},{16,24},{24,16},{32,40},{40,32},{48,56},{56,48},{64,72... | collective-permute-start | bytes 786440 | tf_op jit(solution)/shard_map/ppermute | solution.py:16
  30.2 7.9 %all-to-all-start.1 = ((bf16[4,64,256]{2,1,0:T(8,128)(2,1)}), bf16[4,64,256]{2,1,0:T(8,128)(2,1)S(1)}, u32[]{:S(2)}, u32[]{:S(2)}) async-start(bf16[4,64,256]{2,1,0:T(8,128)(2,1)} %broadcast_in_dim.5), calls=%async_computation.1 | async-start | bytes 262144 | tf_op jit(solution)/shard_map/all_to_all | solution.py:125
  33.6 11.7 %collective-permute-start.5 = (bf16[512,256]{1,0:T(8,128)(2,1)S(1)}, bf16[512,256]{1,0:T(8,128)(2,1)S(1)}, u32[]{:S(2)}, u32[]{:S(2)}) collective-permute-start(bf16[512,256]{1,0:T(8,128)(2,1)S(1)} %slice.22), channel_id=1, source_target_pairs={{0,16},{8,24},{16,0},{24,8},{32,48},{40,56},{48,32},{56,40},{64,80... | collective-permute-start | bytes 786440 | tf_op jit(solution)/shard_map/ppermute | solution.py:16
  38.9 42.9 %collective-permute-start = (bf16[576,256]{1,0:T(8,128)(2,1)}, bf16[576,256]{1,0:T(8,128)(2,1)S(1)}, u32[]{:S(2)}, u32[]{:S(2)}) collective-permute-start(bf16[576,256]{1,0:T(8,128)(2,1)} %pad_maximum_fusion.2), channel_id=1, source_target_pairs={{0,32},{8,40},{16,48},{24,56},{32,0},{40,8},{48,16},{56,24},{64,96... | collective-permute-start | bytes 884744 | tf_op jit(solution)/shard_map/ppermute | solution.py:16
  41.8 40.0 %collective-permute-start.1 = (bf16[576,256]{1,0:T(8,128)(2,1)}, bf16[576,256]{1,0:T(8,128)(2,1)S(1)}, u32[]{:S(2)}, u32[]{:S(2)}) collective-permute-start(bf16[576,256]{1,0:T(8,128)(2,1)} %pad_maximum_fusion.2), channel_id=1, source_target_pairs={{0,64},{8,72},{16,80},{24,88},{32,96},{40,104},{48,112},{56,120},{... | collective-permute-start | bytes 884744 | tf_op jit(solution)/shard_map/ppermute | solution.py:16
  45.3 27.7 %collective-permute-start.6 = (bf16[64,256]{1,0:T(8,128)(2,1)S(1)}, bf16[64,256]{1,0:T(8,128)(2,1)S(1)}, u32[]{:S(2)}, u32[]{:S(2)}) collective-permute-start(bf16[64,256]{1,0:T(8,128)(2,1)S(1)} %reduce_sum.12), channel_id=1, source_target_pairs={{0,96},{8,104},{16,112},{24,120},{32,64},{40,72},{48,80},{56,88},{... | collective-permute-start | bytes 98312 | tf_op jit(solution)/shard_map/ppermute | solution.py:16
  73.0 30.9 %copy-start.3 = (f32[4]{0:T(128)S(1)}, f32[4]{0:T(128)}, u32[]{:S(2)}) copy-start(f32[4]{0:T(128)} %param.11) | copy-start | bytes 52
  74.8 36.8 %all-to-all-start.2 = ((bf16[8,64,512]{2,1,0:T(8,128)(2,1)}), bf16[8,64,512]{2,1,0:T(8,128)(2,1)S(1)}, u32[]{:S(2)}, u32[]{:S(2)}) async-start(bf16[8,64,512]{2,1,0:T(8,128)(2,1)} %pad_maximum_fusion.1), calls=%async_computation.2 | async-start | bytes 1048576 | tf_op jit(solution)/shard_map/all_to_all | solution.py:115
  81.8 22.1 %collective-permute-start.7 = (bf16[64,256]{1,0:T(8,128)(2,1)S(1)}, bf16[64,256]{1,0:T(8,128)(2,1)S(1)}, u32[]{:S(2)}, u32[]{:S(2)}) collective-permute-start(bf16[64,256]{1,0:T(8,128)(2,1)S(1)} %fusion.3), channel_id=1, source_target_pairs={{0,128},{8,136},{16,144},{24,152},{32,160},{40,168},{48,176},{56,1... | collective-permute-start | bytes 98312 | tf_op jit(solution)/shard_map/ppermute | solution.py:16
  93.0 14.5 %collective-permute-start.8 = (bf16[64,256]{1,0:T(8,128)(2,1)S(1)}, bf16[64,256]{1,0:T(8,128)(2,1)S(1)}, u32[]{:S(2)}, u32[]{:S(2)}) collective-permute-start(bf16[64,256]{1,0:T(8,128)(2,1)S(1)} %fusion.3), channel_id=1, source_target_pairs={{0,256},{8,264},{16,272},{24,280},{32,288},{40,296},{48,304},{56,3... | collective-permute-start | bytes 98312 | tf_op jit(solution)/shard_map/ppermute | solution.py:16
  101.9 9.7 %collective-permute-start.9 = (bf16[64,256]{1,0:T(8,128)(2,1)S(1)}, bf16[64,256]{1,0:T(8,128)(2,1)S(1)}, u32[]{:S(2)}, u32[]{:S(2)}) collective-permute-start(bf16[64,256]{1,0:T(8,128)(2,1)S(1)} %fusion.3), channel_id=1, source_target_pairs={{0,384},{8,392},{16,400},{24,408},{32,416},{40,424},{48,432},{56,4... | collective-permute-start | bytes 98312 | tf_op jit(solution)/shard_map/ppermute | solution.py:16

commit v3 on v2

--- a/solution.py
+++ b/solution.py
@@ -18,11 +18,14 @@
 
 def attend_kernel(count, first, final, bias_ref, q_ref, *refs):
     k_refs, v_refs, refs = refs[: 2 * count : 2], refs[1 : 2 * count : 2], refs[2 * count :]
+    refs, turned = refs[:-count], refs[-count:]
     if not first:
         acc_in, stat_in, refs = refs[0], refs[1], refs[2:]
     scale = HD**-0.5 * LOG2E
     rows, heads = q_ref.shape[0], q_ref.shape[1] // HD
-    tile = 256
+    tile = 512
+    for j in range(count):
+        turned[j][...] = k_refs[j][...].T
     for head in range(heads):
         for start in range(0, rows, tile):
             part, cols = pl.ds(start, tile), pl.ds(head * HD, HD)
@@ -30,7 +33,7 @@
             scores, top = [], None
             for j in range(count):
                 s = lax.dot_general(
-                    query, k_refs[j][...], (((1,), (1,)), ((), ())), preferred_element_type=jnp.float32
+                    query, turned[j][...], (((1,), (0,)), ((), ())), preferred_element_type=jnp.float32
                 )
                 bias = bias_ref[j, head] * LOG2E
                 most = jnp.max(s, axis=-1, keepdims=True) * scale + bias
@@ -66,16 +69,15 @@
 def attend(state, queries, blocks, biases, final=False):
     rows, heads = queries.shape[0], biases.shape[1]
     width, count, first = heads * HD, len(blocks), state is None
-    steps = 2
 
-    def by_rows(columns):
-        return pl.BlockSpec((rows // steps, columns), lambda i: (i, 0))
+    def whole(columns):
+        return pl.BlockSpec((rows, columns), lambda i: (0, 0))
 
     def columns_at(size, place):
         return pl.BlockSpec((size, HD), lambda i: (0, place))
 
-    state_specs = (by_rows(width), by_rows(2 * heads))
-    in_specs = [pl.BlockSpec(memory_space=pltpu.SMEM), by_rows(width)]
+    state_specs = (whole(width), whole(2 * heads))
+    in_specs = [pl.BlockSpec(memory_space=pltpu.SMEM), whole(width)]
     args = [biases, queries]
     for size, key_array, key_place, value_array, value_place in blocks:
         in_specs += [columns_at(size, key_place), columns_at(size, value_place)]
@@ -84,16 +86,17 @@
         in_specs += state_specs
         args += state
     if final:
-        out_shape, out_specs = jax.ShapeDtypeStruct((rows, width), jnp.bfloat16), by_rows(width)
+        out_shape, out_specs = jax.ShapeDtypeStruct((rows, width), jnp.bfloat16), whole(width)
     else:
         out_shape = tuple(jax.ShapeDtypeStruct((rows, n), jnp.float32) for n in (width, 2 * heads))
         out_specs = state_specs
     return pl.pallas_call(
         functools.partial(attend_kernel, count, first, final),
-        grid=(steps,),
+        grid=(1,),
         in_specs=in_specs,
         out_specs=out_specs,
         out_shape=out_shape,
+        scratch_shapes=[pltpu.VMEM((HD, block[0]), jnp.bfloat16) for block in blocks],
         compiler_params=pltpu.CompilerParams(vmem_limit_bytes=24 * 1024 * 1024),
     )(*args)
 
@@ -128,7 +131,12 @@
         (partners[0] == jnp.bitwise_xor(block_index, 1 << bit)).astype(jnp.float32) for bit in range(bits)
     ]
     bias = jnp.concatenate(
-        [jnp.zeros_like(anchor_bias)[None], jnp.stack(chosen) @ level_bias.T, anchor_bias[None]], axis=0
+        [
+            jnp.zeros_like(anchor_bias)[None],
+            jnp.sum(jnp.stack(chosen)[:, None, :] * level_bias[None], axis=2),
+            anchor_bias[None],
+        ],
+        axis=0,
     )
 
     kv_shard = jnp.concatenate([by_head(keys), by_head(values)], axis=2)
@@ -149,7 +157,7 @@
     )
     carried = jnp.concatenate([kv, plane], axis=0)
     level3, level2, diagonal = swap(carried, 8), swap(carried, 4), swap(carried[rows:], 12)
-    shard4, shard5, state, diagonal = after((shard4, shard5, state, diagonal))
+    shard5, shard4, state = after((shard5, shard4, state))
     far = to_heads(jnp.concatenate([shard4, shard5], axis=2))
     mine = plane + level2[rows:] + level3[rows:] + diagonal
     anchors = mine + swap(mine, 16) + swap(mine, 32) + swap(mine, 48)

time: 139 us -> 130 us (0.935)
  the two profiles are of different devices: /device:TPU:96 before, /device:TPU:32 now
where the time goes in v3:
time: 130 us; the launch traced here: 129 us
  starting transfers between devices  71.6 us (55%)
  waiting for transfers between devices  20.3 us (16%)
  blocking collectives  16.8 us (13%)
  Pallas kernels  12.8 us (10%)
  other arithmetic  4.45 us (3%)
  local copies, waits for them, and re-layouts  2.79 us (2%)
    ppermute x10, starting transfers between devices, swap(): lax.ppermute(value, 'seq', [(i, i ^ bit) for i in range(lax.axis_size('se...  54.1 us
    ppermute x10, waiting for transfers between devices, swap(): lax.ppermute(value, 'seq', [(i, i ^ bit) for i in range(lax.axis_size('se...  20.3 us
    all_to_all x1, blocking collectives, on_device(): lax.all_to_all(result, 'head', split_axis=0, concat_axis=1, tiled=True)  16.8 us
    all_to_all x2, starting transfers between devices, to_heads(): lax.all_to_all(array, 'head', split_axis=0, concat_axis=0, tiled=True)  14.3 us
    pallas_call x2, Pallas kernels, attend(): pl.pallas_call(functools.partial(attend_kernel, count, first, final), gri...  12.8 us
    all_to_all x1, starting transfers between devices, from_four(): lax.all_to_all(copies, 'seq', split_axis=0, concat_axis=0, axis_index_gro...  3.32 us
  transfers between devices with their start and end apart: 13, of which 3 were waited for; matrix products, arithmetic and copies ran while one was open for 3% of the time, Pallas kernels for 4%

profile of v3, /device:TPU:32, one launch (start us, length us, event | category | flops | bytes accessed | tf_op | source)
XLA Modules:
  0.0 129.3 jit_solution(7598022017456792967)
XLA Ops:
  0.0 1.1 copy.23
  1.2 1.0 pad_maximum_fusion
  2.2 7.1 %all-to-all-start = ((bf16[8,64,768]{2,1,0:T(8,128)(2,1)}), bf16[8,64,768]{2,1,0:T(8,128)(2,1)S(1)}, u32[]{:S(2)}, u32[]{:S(2)}) async-start(bf16[8,64,768]{2,1,0:T(8,128)(2,1)} %pad_maximum_fusion), calls=%async_computation | async-start | bytes 1572864 | tf_op jit(solution)/shard_map/all_to_all | solution.py:118
  9.3 0.7 pad_maximum_fusion.3
  10.0 9.1 %collective-permute-start.3 = (bf16[8,64,256]{2,1,0:T(8,128)(2,1)}, bf16[8,64,256]{2,1,0:T(8,128)(2,1)}, u32[]{:S(2)}, u32[]{:S(2)}) collective-permute-start(bf16[8,64,256]{2,1,0:T(8,128)(2,1)} %pad_maximum_fusion.3), channel_id=1, source_target_pairs={{0,128},{8,136},{16,144},{24,152},{32,160},{40,168},{48,176},{56,1... | collective-permute-start | bytes 786440 | tf_op jit(solution)/shard_map/ppermute | solution.py:16
  19.1 10.0 %collective-permute-start.2 = (bf16[8,64,256]{2,1,0:T(8,128)(2,1)}, bf16[8,64,256]{2,1,0:T(8,128)(2,1)}, u32[]{:S(2)}, u32[]{:S(2)}) collective-permute-start(bf16[8,64,256]{2,1,0:T(8,128)(2,1)} %pad_maximum_fusion.3), channel_id=1, source_target_pairs={{0,256},{8,264},{16,272},{24,280},{32,288},{40,296},{48,304},{56,3... | collective-permute-start | bytes 786440 | tf_op jit(solution)/shard_map/ppermute | solution.py:16
  30.1 3.3 %all-to-all-start.1 = ((bf16[4,64,256]{2,1,0:T(8,128)(2,1)}), bf16[4,64,256]{2,1,0:T(8,128)(2,1)S(1)}, u32[]{:S(2)}, u32[]{:S(2)}) async-start(bf16[4,64,256]{2,1,0:T(8,128)(2,1)} %broadcast_in_dim.5), calls=%async_computation.1 | async-start | bytes 262144 | tf_op jit(solution)/shard_map/all_to_all | solution.py:128
  33.4 2.4 %collective-permute-start.4 = (bf16[512,256]{1,0:T(8,128)(2,1)S(1)}, bf16[512,256]{1,0:T(8,128)(2,1)S(1)}, u32[]{:S(2)}, u32[]{:S(2)}) collective-permute-start(bf16[512,256]{1,0:T(8,128)(2,1)S(1)} %slice.22), channel_id=1, source_target_pairs={{0,8},{8,0},{16,24},{24,16},{32,40},{40,32},{48,56},{56,48},{64,72... | collective-permute-start | bytes 786440 | tf_op jit(solution)/shard_map/ppermute | solution.py:16
  35.8 3.6 %collective-permute-start.5 = (bf16[512,256]{1,0:T(8,128)(2,1)S(1)}, bf16[512,256]{1,0:T(8,128)(2,1)S(1)}, u32[]{:S(2)}, u32[]{:S(2)}) collective-permute-start(bf16[512,256]{1,0:T(8,128)(2,1)S(1)} %slice.22), channel_id=1, source_target_pairs={{0,16},{8,24},{16,0},{24,8},{32,48},{40,56},{48,32},{56,40},{64,80... | collective-permute-start | bytes 786440 | tf_op jit(solution)/shard_map/ppermute | solution.py:16
  40.2 3.4 %collective-permute-start.1 = (bf16[576,256]{1,0:T(8,128)(2,1)}, bf16[576,256]{1,0:T(8,128)(2,1)S(1)}, u32[]{:S(2)}, u32[]{:S(2)}) collective-permute-start(bf16[576,256]{1,0:T(8,128)(2,1)} %pad_maximum_fusion.2), channel_id=1, source_target_pairs={{0,64},{8,72},{16,80},{24,88},{32,96},{40,104},{48,112},{56,120},{... | collective-permute-start | bytes 884744 | tf_op jit(solution)/shard_map/ppermute | solution.py:16
  43.6 2.9 %collective-permute-start = (bf16[576,256]{1,0:T(8,128)(2,1)}, bf16[576,256]{1,0:T(8,128)(2,1)S(1)}, u32[]{:S(2)}, u32[]{:S(2)}) collective-permute-start(bf16[576,256]{1,0:T(8,128)(2,1)} %pad_maximum_fusion.2), channel_id=1, source_target_pairs={{0,32},{8,40},{16,48},{24,56},{32,0},{40,8},{48,16},{56,24},{64,96... | collective-permute-start | bytes 884744 | tf_op jit(solution)/shard_map/ppermute | solution.py:16
  46.6 2.9 %collective-permute-start.6 = (bf16[64,256]{1,0:T(8,128)(2,1)S(1)}, bf16[64,256]{1,0:T(8,128)(2,1)S(1)}, u32[]{:S(2)}, u32[]{:S(2)}) collective-permute-start(bf16[64,256]{1,0:T(8,128)(2,1)S(1)} %reduce_sum.22), channel_id=1, source_target_pairs={{0,96},{8,104},{16,112},{24,120},{32,64},{40,72},{48,80},{56,88},{... | collective-permute-start | bytes 98312 | tf_op jit(solution)/shard_map/ppermute | solution.py:16
  49.6 5.6 %shard_map.73 = (f32[512,512]{1,0:T(8,128)S(1)}, f32[512,8]{1,0:T(8,128)S(1)}) custom-call(f32[3,4]{1,0:T(4,128)S(1)} %pad_slice_fusion.bias_ref, bf16[512,768]{1,0:T(8,128)(2,1)S(1)} %bitcast.30, bf16[512,768]{1,0:T(8,128)(2,1)S(1)} %bitcast.31, bf16[512,768]{1,0:T(8,128)(2,1)S(1)} %bitcast.32, bf16[512,256]{1,0:T(8,128)(2,1)S(1)} %collective-permute-done.4.refs_2_.refs_3_, ...), custom_call_target="tpu_custom_call" | custom-call | tf_op jit(solution)/shard_map/pallas_call | solution.py:93
  55.2 1.9 %pad_maximum_fusion.1 = bf16[8,64,512]{2,1,0:T(8,128)(2,1)} fusion(bf16[8,64,256]{2,1,0:T(8,128)(2,1)} %collective-permute-done.2, bf16[8,64,256]{2,1,0:T(8,128)(2,1)} %collective-permute-done.3), kind=kLoop, calls=%fused_computation.3 | loop fusion | flops 1048576 | bytes 1048576 | tf_op jit(solution)/shard_map/concatenate | solution.py:161
  57.1 7.2 %all-to-all-start.2 = ((bf16[8,64,512]{2,1,0:T(8,128)(2,1)}), bf16[8,64,512]{2,1,0:T(8,128)(2,1)S(1)}, u32[]{:S(2)}, u32[]{:S(2)}) async-start(bf16[8,64,512]{2,1,0:T(8,128)(2,1)} %pad_maximum_fusion.1), calls=%async_computation.2 | async-start | bytes 1048576 | tf_op jit(solution)/shard_map/all_to_all | solution.py:118
  64.3 12.7 %collective-permute-done.6 = bf16[64,256]{1,0:T(8,128)(2,1)S(1)} collective-permute-done((bf16[64,256]{1,0:T(8,128)(2,1)S(1)}, bf16[64,256]{1,0:T(8,128)(2,1)S(1)}, u32[]{:S(2)}, u32[]{:S(2)}) %collective-permute-start.6) | collective-permute-done | bytes 32800 | tf_op jit(solution)/shard_map/ppermute | solution.py:16
  77.0 9.8 %collective-permute-start.9 = (bf16[64,256]{1,0:T(8,128)(2,1)S(1)}, bf16[64,256]{1,0:T(8,128)(2,1)S(1)}, u32[]{:S(2)}, u32[]{:S(2)}) collective-permute-start(bf16[64,256]{1,0:T(8,128)(2,1)S(1)} %fusion.3), channel_id=1, source_target_pairs={{0,384},{8,392},{16,400},{24,408},{32,416},{40,424},{48,432},{56,4... | collective-permute-start | bytes 98312 | tf_op jit(solution)/shard_map/ppermute | solution.py:16
  86.8 7.9 %collective-permute-start.8 = (bf16[64,256]{1,0:T(8,128)(2,1)S(1)}, bf16[64,256]{1,0:T(8,128)(2,1)S(1)}, u32[]{:S(2)}, u32[]{:S(2)}) collective-permute-start(bf16[64,256]{1,0:T(8,128)(2,1)S(1)} %fusion.3), channel_id=1, source_target_pairs={{0,256},{8,264},{16,272},{24,280},{32,288},{40,296},{48,304},{56,3... | collective-permute-start | bytes 98312 | tf_op jit(solution)/shard_map/ppermute | solution.py:16
  94.7 2.1 %collective-permute-start.7 = (bf16[64,256]{1,0:T(8,128)(2,1)S(1)}, bf16[64,256]{1,0:T(8,128)(2,1)S(1)}, u32[]{:S(2)}, u32[]{:S(2)}) collective-permute-start(bf16[64,256]{1,0:T(8,128)(2,1)S(1)} %fusion.3), channel_id=1, source_target_pairs={{0,128},{8,136},{16,144},{24,152},{32,160},{40,168},{48,176},{56,1... | collective-permute-start | bytes 98312 | tf_op jit(solution)/shard_map/ppermute | solution.py:16
  96.9 5.2 %collective-permute-done.8 = bf16[64,256]{1,0:T(8,128)(2,1)S(1)} collective-permute-done((bf16[64,256]{1,0:T(8,128)(2,1)S(1)}, bf16[64,256]{1,0:T(8,128)(2,1)S(1)}, u32[]{:S(2)}, u32[]{:S(2)}) %collective-permute-start.8) | collective-permute-done | bytes 32800 | tf_op jit(solution)/shard_map/ppermute | solution.py:16
  102.0 2.4 %collective-permute-done.7 = bf16[64,256]{1,0:T(8,128)(2,1)S(1)} collective-permute-done((bf16[64,256]{1,0:T(8,128)(2,1)S(1)}, bf16[64,256]{1,0:T(8,128)(2,1)S(1)}, u32[]{:S(2)}, u32[]{:S(2)}) %collective-permute-start.7) | collective-permute-done | bytes 32800 | tf_op jit(solution)/shard_map/ppermute | solution.py:16
  104.5 7.1 %shard_map.74 = bf16[512,512]{1,0:T(8,128)(2,1)S(1)} custom-call(f32[5,4]{1,0:T(8,128)S(1)} %slice.17.bias_ref, bf16[512,768]{1,0:T(8,128)(2,1)S(1)} %bitcast.33, bf16[576,256]{1,0:T(8,128)(2,1)S(1)} %collective-permute-done.refs_0_.refs_1_, bf16[576,256]{1,0:T(8,128)(2,1)S(1)} %collective-permute-done.refs_0_.refs_1_, ...), custom_call_target="tpu_custom_call" | custom-call | tf_op jit(solution)/shard_map/pallas_call | solution.py:93
  111.6 16.8 %all_to_all.34 = bf16[8,64,512]{2,1,0:T(8,128)(2,1)S(1)} all-to-all(bf16[8,64,512]{2,1,0:T(8,128)(2,1)S(1)} %bitcast.38), channel_id=1, replica_groups=mesh['seq'=64,'head'=8] {'head'}, dimensions={0} | all-to-all | bytes 1048576 | tf_op jit(solution)/shard_map/all_to_all | solution.py:178
  128.4 0.8 copy.19
  (38 shorter events, 1.9 us)
Async XLA Ops:
  0.0 1.1 copy-start
  0.0 1.1 copy-start.1
  2.2 27.0 %copy-start.5 = (s32[64]{0:T(128)S(1)}, s32[64]{0:T(128)}, u32[]{:S(2)}) copy-start(s32[64]{0:T(128)} %param.13) | copy-start | bytes 772
  2.2 27.0 %all-to-all-start = ((bf16[8,64,768]{2,1,0:T(8,128)(2,1)}), bf16[8,64,768]{2,1,0:T(8,128)(2,1)S(1)}, u32[]{:S(2)}, u32[]{:S(2)}) async-start(bf16[8,64,768]{2,1,0:T(8,128)(2,1)} %pad_maximum_fusion), calls=%async_computation | async-start | bytes 1572864 | tf_op jit(solution)/shard_map/all_to_all | solution.py:118
  9.2 26.5 %copy-start.4 = (s32[1,6]{1,0:T(1,128)S(1)}, s32[1,6]{1,0:T(1,128)}, u32[]{:S(2)}) copy-start(s32[1,6]{1,0:T(1,128)} %param.12) | copy-start | bytes 76
  10.0 45.2 %collective-permute-start.3 = (bf16[8,64,256]{2,1,0:T(8,128)(2,1)}, bf16[8,64,256]{2,1,0:T(8,128)(2,1)}, u32[]{:S(2)}, u32[]{:S(2)}) collective-permute-start(bf16[8,64,256]{2,1,0:T(8,128)(2,1)} %pad_maximum_fusion.3), channel_id=1, source_target_pairs={{0,128},{8,136},{16,144},{24,152},{32,160},{40,168},{48,176},{56,1... | collective-permute-start | bytes 786440 | tf_op jit(solution)/shard_map/ppermute | solution.py:16
  19.1 36.1 %collective-permute-start.2 = (bf16[8,64,256]{2,1,0:T(8,128)(2,1)}, bf16[8,64,256]{2,1,0:T(8,128)(2,1)}, u32[]{:S(2)}, u32[]{:S(2)}) collective-permute-start(bf16[8,64,256]{2,1,0:T(8,128)(2,1)} %pad_maximum_fusion.3), channel_id=1, source_target_pairs={{0,256},{8,264},{16,272},{24,280},{32,288},{40,296},{48,304},{56,3... | collective-permute-start | bytes 786440 | tf_op jit(solution)/shard_map/ppermute | solution.py:16
  29.1 17.4 %copy-start.2 = (f32[4,6]{1,0:T(4,128)S(1)}, f32[4,6]{1,0:T(4,128)}, u32[]{:S(2)}) copy-start(f32[4,6]{1,0:T(4,128)} %param.10) | copy-start | bytes 292
  30.1 9.4 %all-to-all-start.1 = ((bf16[4,64,256]{2,1,0:T(8,128)(2,1)}), bf16[4,64,256]{2,1,0:T(8,128)(2,1)S(1)}, u32[]{:S(2)}, u32[]{:S(2)}) async-start(bf16[4,64,256]{2,1,0:T(8,128)(2,1)} %broadcast_in_dim.5), calls=%async_computation.1 | async-start | bytes 262144 | tf_op jit(solution)/shard_map/all_to_all | solution.py:128
  33.4 10.2 %collective-permute-start.4 = (bf16[512,256]{1,0:T(8,128)(2,1)S(1)}, bf16[512,256]{1,0:T(8,128)(2,1)S(1)}, u32[]{:S(2)}, u32[]{:S(2)}) collective-permute-start(bf16[512,256]{1,0:T(8,128)(2,1)S(1)} %slice.22), channel_id=1, source_target_pairs={{0,8},{8,0},{16,24},{24,16},{32,40},{40,32},{48,56},{56,48},{64,72... | collective-permute-start | bytes 786440 | tf_op jit(solution)/shard_map/ppermute | solution.py:16
  35.8 10.8 %collective-permute-start.5 = (bf16[512,256]{1,0:T(8,128)(2,1)S(1)}, bf16[512,256]{1,0:T(8,128)(2,1)S(1)}, u32[]{:S(2)}, u32[]{:S(2)}) collective-permute-start(bf16[512,256]{1,0:T(8,128)(2,1)S(1)} %slice.22), channel_id=1, source_target_pairs={{0,16},{8,24},{16,0},{24,8},{32,48},{40,56},{48,32},{56,40},{64,80... | collective-permute-start | bytes 786440 | tf_op jit(solution)/shard_map/ppermute | solution.py:16
  40.2 36.8 %collective-permute-start.1 = (bf16[576,256]{1,0:T(8,128)(2,1)}, bf16[576,256]{1,0:T(8,128)(2,1)S(1)}, u32[]{:S(2)}, u32[]{:S(2)}) collective-permute-start(bf16[576,256]{1,0:T(8,128)(2,1)} %pad_maximum_fusion.2), channel_id=1, source_target_pairs={{0,64},{8,72},{16,80},{24,88},{32,96},{40,104},{48,112},{56,120},{... | collective-permute-start | bytes 884744 | tf_op jit(solution)/shard_map/ppermute | solution.py:16
  43.6 33.4 %collective-permute-start = (bf16[576,256]{1,0:T(8,128)(2,1)}, bf16[576,256]{1,0:T(8,128)(2,1)S(1)}, u32[]{:S(2)}, u32[]{:S(2)}) collective-permute-start(bf16[576,256]{1,0:T(8,128)(2,1)} %pad_maximum_fusion.2), channel_id=1, source_target_pairs={{0,32},{8,40},{16,48},{24,56},{32,0},{40,8},{48,16},{56,24},{64,96... | collective-permute-start | bytes 884744 | tf_op jit(solution)/shard_map/ppermute | solution.py:16
  46.6 30.3 %collective-permute-start.6 = (bf16[64,256]{1,0:T(8,128)(2,1)S(1)}, bf16[64,256]{1,0:T(8,128)(2,1)S(1)}, u32[]{:S(2)}, u32[]{:S(2)}) collective-permute-start(bf16[64,256]{1,0:T(8,128)(2,1)S(1)} %reduce_sum.22), channel_id=1, source_target_pairs={{0,96},{8,104},{16,112},{24,120},{32,64},{40,72},{48,80},{56,88},{... | collective-permute-start | bytes 98312 | tf_op jit(solution)/shard_map/ppermute | solution.py:16
  55.2 41.6 %copy-start.3 = (f32[4]{0:T(128)S(1)}, f32[4]{0:T(128)}, u32[]{:S(2)}) copy-start(f32[4]{0:T(128)} %param.11) | copy-start | bytes 52
  57.1 47.4 %all-to-all-start.2 = ((bf16[8,64,512]{2,1,0:T(8,128)(2,1)}), bf16[8,64,512]{2,1,0:T(8,128)(2,1)S(1)}, u32[]{:S(2)}, u32[]{:S(2)}) async-start(bf16[8,64,512]{2,1,0:T(8,128)(2,1)} %pad_maximum_fusion.1), calls=%async_computation.2 | async-start | bytes 1048576 | tf_op jit(solution)/shard_map/all_to_all | solution.py:118
  77.0 19.9 %collective-permute-start.9 = (bf16[64,256]{1,0:T(8,128)(2,1)S(1)}, bf16[64,256]{1,0:T(8,128)(2,1)S(1)}, u32[]{:S(2)}, u32[]{:S(2)}) collective-permute-start(bf16[64,256]{1,0:T(8,128)(2,1)S(1)} %fusion.3), channel_id=1, source_target_pairs={{0,384},{8,392},{16,400},{24,408},{32,416},{40,424},{48,432},{56,4... | collective-permute-start | bytes 98312 | tf_op jit(solution)/shard_map/ppermute | solution.py:16
  86.8 15.2 %collective-permute-start.8 = (bf16[64,256]{1,0:T(8,128)(2,1)S(1)}, bf16[64,256]{1,0:T(8,128)(2,1)S(1)}, u32[]{:S(2)}, u32[]{:S(2)}) collective-permute-start(bf16[64,256]{1,0:T(8,128)(2,1)S(1)} %fusion.3), channel_id=1, source_target_pairs={{0,256},{8,264},{16,272},{24,280},{32,288},{40,296},{48,304},{56,3... | collective-permute-start | bytes 98312 | tf_op jit(solution)/shard_map/ppermute | solution.py:16
  94.7 9.8 %collective-permute-start.7 = (bf16[64,256]{1,0:T(8,128)(2,1)S(1)}, bf16[64,256]{1,0:T(8,128)(2,1)S(1)}, u32[]{:S(2)}, u32[]{:S(2)}) collective-permute-start(bf16[64,256]{1,0:T(8,128)(2,1)S(1)} %fusion.3), channel_id=1, source_target_pairs={{0,128},{8,136},{16,144},{24,152},{32,160},{40,168},{48,176},{56,1... | collective-permute-start | bytes 98312 | tf_op jit(solution)/shard_map/ppermute | solution.py:16

commit v4 on v3

--- a/solution.py
+++ b/solution.py
@@ -155,12 +155,16 @@
         [(rows, qkv, places, qkv, places + 1), (rows, near, 0, near, 1), (rows, level1, 0, level1, 1)],
         bias[0:3],
     )
-    carried = jnp.concatenate([kv, plane], axis=0)
-    level3, level2, diagonal = swap(carried, 8), swap(carried, 4), swap(carried[rows:], 12)
-    shard5, shard4, state = after((shard5, shard4, state))
+    plane16, plane32, plane48 = swap(plane, 16), swap(plane, 32), swap(plane, 48)
+    kv_2, plane = after((kv, plane))
+    level3, level2 = swap(kv_2, 8), swap(kv_2, 4)
+    shard4, shard5, state, plane48, plane32, plane16 = after(
+        (shard4, shard5, state, plane48, plane32, plane16)
+    )
     far = to_heads(jnp.concatenate([shard4, shard5], axis=2))
-    mine = plane + level2[rows:] + level3[rows:] + diagonal
-    anchors = mine + swap(mine, 16) + swap(mine, 32) + swap(mine, 48)
+    strided = plane + plane16 + plane32 + plane48
+    strided, level2, level3 = after((strided, level2, level3))
+    anchors = strided + swap(strided, 4) + swap(strided, 8) + swap(strided, 12)
     count = anchors.shape[0]
     result = attend(
         state,

time: 130 us -> 123 us (0.946)
  the two profiles are of different devices: /device:TPU:32 before, /device:TPU:8 now
where the time goes in v4:
time: 123 us
  starting transfers between devices  75.4 us (61%)
  blocking collectives  16.8 us (14%)
  Pallas kernels  12.8 us (10%)
  waiting for transfers between devices  10 us (8%)
  other arithmetic  4.34 us (4%)
  local copies, waits for them, and re-layouts  2.78 us (2%)
    ppermute x12, starting transfers between devices, swap(): lax.ppermute(value, 'seq', [(i, i ^ bit) for i in range(lax.axis_size('se...  58.3 us
    all_to_all x1, blocking collectives, on_device(): lax.all_to_all(result, 'head', split_axis=0, concat_axis=1, tiled=True)  16.8 us
    all_to_all x2, starting transfers between devices, to_heads(): lax.all_to_all(array, 'head', split_axis=0, concat_axis=0, tiled=True)  13.1 us
    pallas_call x2, Pallas kernels, attend(): pl.pallas_call(functools.partial(attend_kernel, count, first, final), gri...  12.8 us
    ppermute x12, waiting for transfers between devices, swap(): lax.ppermute(value, 'seq', [(i, i ^ bit) for i in range(lax.axis_size('se...  6.21 us
    all_to_all x1, starting transfers between devices, from_four(): lax.all_to_all(copies, 'seq', split_axis=0, concat_axis=0, axis_index_gro...  3.97 us
    all_to_all x1, waiting for transfers between devices, from_four(): lax.all_to_all(copies, 'seq', split_axis=0, concat_axis=0, axis_index_gro...  3.79 us
  transfers between devices with their start and end apart: 15, of which 5 were waited for; matrix products, arithmetic and copies ran while one was open for 4% of the time, Pallas kernels for 5%

profile of v4, /device:TPU:8, one launch (start us, length us, event | category | flops | bytes accessed | tf_op | source)
XLA Modules:
  0.0 122.6 jit_solution(16216391412649931929)
XLA Ops:
  0.0 1.1 copy.23
  1.2 1.0 pad_maximum_fusion
  2.2 6.2 %all-to-all-start = ((bf16[8,64,768]{2,1,0:T(8,128)(2,1)}), bf16[8,64,768]{2,1,0:T(8,128)(2,1)S(1)}, u32[]{:S(2)}, u32[]{:S(2)}) async-start(bf16[8,64,768]{2,1,0:T(8,128)(2,1)} %pad_maximum_fusion), calls=%async_computation | async-start | bytes 1572864 | tf_op jit(solution)/shard_map/all_to_all | solution.py:118
  8.4 9.1 %collective-permute-start = (bf16[8,64,256]{2,1,0:T(8,128)(2,1)S(1)}, bf16[8,64,256]{2,1,0:T(8,128)(2,1)S(1)}, u32[]{:S(2)}, u32[]{:S(2)}) collective-permute-start(bf16[8,64,256]{2,1,0:T(8,128)(2,1)S(1)} %pad_maximum_fusion.2), channel_id=1, source_target_pairs={{0,128},{8,136},{16,144},{24,152},{32,160},{40,168},{48,176},{56,1... | collective-permute-start | bytes 786440 | tf_op jit(solution)/shard_map/ppermute | solution.py:16
  17.5 10.9 %collective-permute-start.1 = (bf16[8,64,256]{2,1,0:T(8,128)(2,1)S(1)}, bf16[8,64,256]{2,1,0:T(8,128)(2,1)}, u32[]{:S(2)}, u32[]{:S(2)}) collective-permute-start(bf16[8,64,256]{2,1,0:T(8,128)(2,1)S(1)} %pad_maximum_fusion.2), channel_id=1, source_target_pairs={{0,256},{8,264},{16,272},{24,280},{32,288},{40,296},{48,304},{56,3... | collective-permute-start | bytes 786440 | tf_op jit(solution)/shard_map/ppermute | solution.py:16
  28.5 1.9 %collective-permute-start.2 = (bf16[512,256]{1,0:T(8,128)(2,1)S(1)}, bf16[512,256]{1,0:T(8,128)(2,1)S(1)}, u32[]{:S(2)}, u32[]{:S(2)}) collective-permute-start(bf16[512,256]{1,0:T(8,128)(2,1)S(1)} %slice.14), channel_id=1, source_target_pairs={{0,8},{8,0},{16,24},{24,16},{32,40},{40,32},{48,56},{56,48},{64,72... | collective-permute-start | bytes 786440 | tf_op jit(solution)/shard_map/ppermute | solution.py:16
  30.5 3.3 %collective-permute-start.3 = (bf16[512,256]{1,0:T(8,128)(2,1)S(1)}, bf16[512,256]{1,0:T(8,128)(2,1)S(1)}, u32[]{:S(2)}, u32[]{:S(2)}) collective-permute-start(bf16[512,256]{1,0:T(8,128)(2,1)S(1)} %slice.14), channel_id=1, source_target_pairs={{0,16},{8,24},{16,0},{24,8},{32,48},{40,56},{48,32},{56,40},{64,80... | collective-permute-start | bytes 786440 | tf_op jit(solution)/shard_map/ppermute | solution.py:16
  34.6 4.0 %all-to-all-start.1 = ((bf16[4,64,256]{2,1,0:T(8,128)(2,1)}), bf16[4,64,256]{2,1,0:T(8,128)(2,1)S(1)}, u32[]{:S(2)}, u32[]{:S(2)}) async-start(bf16[4,64,256]{2,1,0:T(8,128)(2,1)} %broadcast_in_dim.5), calls=%async_computation.1 | async-start | bytes 262144 | tf_op jit(solution)/shard_map/all_to_all | solution.py:128
  38.7 3.8 %all-to-all-done.1 = bf16[4,64,256]{2,1,0:T(8,128)(2,1)S(1)} async-done(((bf16[4,64,256]{2,1,0:T(8,128)(2,1)}), bf16[4,64,256]{2,1,0:T(8,128)(2,1)S(1)}, u32[]{:S(2)}, u32[]{:S(2)}) %all-to-all-start.1) | async-done | bytes 131104 | tf_op jit(solution)/shard_map/all_to_all | solution.py:128
  43.1 5.9 %collective-permute-start.4 = (bf16[64,256]{1,0:T(8,128)(2,1)}, bf16[64,256]{1,0:T(8,128)(2,1)}, u32[]{:S(2)}, u32[]{:S(2)}) collective-permute-start(bf16[64,256]{1,0:T(8,128)(2,1)} %reduce_sum.22), channel_id=1, source_target_pairs={{0,384},{8,392},{16,400},{24,408},{32,416},{40,424},{48,432},{56,4... | collective-permute-start | bytes 98312 | tf_op jit(solution)/shard_map/ppermute | solution.py:16
  49.0 6.8 %collective-permute-start.5 = (bf16[64,256]{1,0:T(8,128)(2,1)}, bf16[64,256]{1,0:T(8,128)(2,1)}, u32[]{:S(2)}, u32[]{:S(2)}) collective-permute-start(bf16[64,256]{1,0:T(8,128)(2,1)} %reduce_sum.22), channel_id=1, source_target_pairs={{0,256},{8,264},{16,272},{24,280},{32,288},{40,296},{48,304},{56,3... | collective-permute-start | bytes 98312 | tf_op jit(solution)/shard_map/ppermute | solution.py:16
  55.9 4.3 %collective-permute-start.6 = (bf16[64,256]{1,0:T(8,128)(2,1)}, bf16[64,256]{1,0:T(8,128)(2,1)}, u32[]{:S(2)}, u32[]{:S(2)}) collective-permute-start(bf16[64,256]{1,0:T(8,128)(2,1)} %reduce_sum.22), channel_id=1, source_target_pairs={{0,128},{8,136},{16,144},{24,152},{32,160},{40,168},{48,176},{56,1... | collective-permute-start | bytes 98312 | tf_op jit(solution)/shard_map/ppermute | solution.py:16
  60.2 5.6 %shard_map.73 = (f32[512,512]{1,0:T(8,128)S(1)}, f32[512,8]{1,0:T(8,128)S(1)}) custom-call(f32[3,4]{1,0:T(4,128)S(1)} %pad_slice_fusion.bias_ref, bf16[512,768]{1,0:T(8,128)(2,1)S(1)} %bitcast.30, bf16[512,768]{1,0:T(8,128)(2,1)S(1)} %bitcast.31, bf16[512,768]{1,0:T(8,128)(2,1)S(1)} %bitcast.32, bf16[512,256]{1,0:T(8,128)(2,1)S(1)} %collective-permute-done.2.refs_2_.refs_3_, ...), custom_call_target="tpu_custom_call" | custom-call | tf_op jit(solution)/shard_map/pallas_call | solution.py:93
  66.7 2.0 %collective-permute-start.7 = (bf16[512,256]{1,0:T(8,128)(2,1)S(1)}, bf16[512,256]{1,0:T(8,128)(2,1)S(1)}, u32[]{:S(2)}, u32[]{:S(2)}) collective-permute-start(bf16[512,256]{1,0:T(8,128)(2,1)S(1)} %slice.14), channel_id=1, source_target_pairs={{0,32},{8,40},{16,48},{24,56},{32,0},{40,8},{48,16},{56,24},{64,96... | collective-permute-start | bytes 786440 | tf_op jit(solution)/shard_map/ppermute | solution.py:16
  68.8 4.6 %collective-permute-start.8 = (bf16[512,256]{1,0:T(8,128)(2,1)S(1)}, bf16[512,256]{1,0:T(8,128)(2,1)S(1)}, u32[]{:S(2)}, u32[]{:S(2)}) collective-permute-start(bf16[512,256]{1,0:T(8,128)(2,1)S(1)} %slice.14), channel_id=1, source_target_pairs={{0,64},{8,72},{16,80},{24,88},{32,96},{40,104},{48,112},{56,120},{... | collective-permute-start | bytes 786440 | tf_op jit(solution)/shard_map/ppermute | solution.py:16
  73.4 1.9 %collective-permute-done.4 = bf16[64,256]{1,0:T(8,128)(2,1)} collective-permute-done((bf16[64,256]{1,0:T(8,128)(2,1)}, bf16[64,256]{1,0:T(8,128)(2,1)}, u32[]{:S(2)}, u32[]{:S(2)}) %collective-permute-start.4) | collective-permute-done | bytes 32800 | tf_op jit(solution)/shard_map/ppermute | solution.py:16
  75.3 1.8 %pad_maximum_fusion.1 = bf16[8,64,512]{2,1,0:T(8,128)(2,1)} fusion(bf16[8,64,256]{2,1,0:T(8,128)(2,1)} %collective-permute-done.1, bf16[8,64,256]{2,1,0:T(8,128)(2,1)S(1)} %collective-permute-done), kind=kLoop, calls=%fused_computation.3 | loop fusion | flops 1048576 | bytes 1048576 | tf_op jit(solution)/shard_map/concatenate | solution.py:164
  77.1 6.9 %all-to-all-start.2 = ((bf16[8,64,512]{2,1,0:T(8,128)(2,1)}), bf16[8,64,512]{2,1,0:T(8,128)(2,1)S(1)}, u32[]{:S(2)}, u32[]{:S(2)}) async-start(bf16[8,64,512]{2,1,0:T(8,128)(2,1)} %pad_maximum_fusion.1), calls=%async_computation.2 | async-start | bytes 1048576 | tf_op jit(solution)/shard_map/all_to_all | solution.py:118
  85.2 1.9 %collective-permute-start.10 = (bf16[64,256]{1,0:T(8,128)(2,1)S(1)}, bf16[64,256]{1,0:T(8,128)(2,1)S(1)}, u32[]{:S(2)}, u32[]{:S(2)}) collective-permute-start(bf16[64,256]{1,0:T(8,128)(2,1)S(1)} %add_add_fusion.1), channel_id=1, source_target_pairs={{0,64},{8,72},{16,80},{24,88},{32,96},{40,104},{48,112},{56,120},{... | collective-permute-start | bytes 98312 | tf_op jit(solution)/shard_map/ppermute | solution.py:16
  87.1 4.9 %collective-permute-start.11 = (bf16[64,256]{1,0:T(8,128)(2,1)S(1)}, bf16[64,256]{1,0:T(8,128)(2,1)S(1)}, u32[]{:S(2)}, u32[]{:S(2)}) collective-permute-start(bf16[64,256]{1,0:T(8,128)(2,1)S(1)} %add_add_fusion.1), channel_id=1, source_target_pairs={{0,96},{8,104},{16,112},{24,120},{32,64},{40,72},{48,80},{56,88},{... | collective-permute-start | bytes 98312 | tf_op jit(solution)/shard_map/ppermute | solution.py:16
  92.0 2.7 %collective-permute-start.9 = (bf16[64,256]{1,0:T(8,128)(2,1)S(1)}, bf16[64,256]{1,0:T(8,128)(2,1)S(1)}, u32[]{:S(2)}, u32[]{:S(2)}) collective-permute-start(bf16[64,256]{1,0:T(8,128)(2,1)S(1)} %add_add_fusion.1), channel_id=1, source_target_pairs={{0,32},{8,40},{16,48},{24,56},{32,0},{40,8},{48,16},{56,24},{64,96... | collective-permute-start | bytes 98312 | tf_op jit(solution)/shard_map/ppermute | solution.py:16
  94.7 3.1 %collective-permute-done.9 = bf16[64,256]{1,0:T(8,128)(2,1)S(1)} collective-permute-done((bf16[64,256]{1,0:T(8,128)(2,1)S(1)}, bf16[64,256]{1,0:T(8,128)(2,1)S(1)}, u32[]{:S(2)}, u32[]{:S(2)}) %collective-permute-start.9) | collective-permute-done | bytes 32800 | tf_op jit(solution)/shard_map/ppermute | solution.py:16
  97.8 7.1 %shard_map.74 = bf16[512,512]{1,0:T(8,128)(2,1)S(1)} custom-call(f32[5,4]{1,0:T(8,128)S(1)} %slice.11.bias_ref, bf16[512,768]{1,0:T(8,128)(2,1)S(1)} %bitcast.33, bf16[512,256]{1,0:T(8,128)(2,1)S(1)} %collective-permute-done.7.refs_0_.refs_1_, bf16[512,256]{1,0:T(8,128)(2,1)S(1)} %collective-permute-done.7.refs_0_.refs_1_, ...), custom_call_target="tpu_custom_call" | custom-call | tf_op jit(solution)/shard_map/pallas_call | solution.py:93
  105.0 16.8 %all_to_all.34 = bf16[8,64,512]{2,1,0:T(8,128)(2,1)S(1)} all-to-all(bf16[8,64,512]{2,1,0:T(8,128)(2,1)S(1)} %bitcast.38), channel_id=1, replica_groups=mesh['seq'=64,'head'=8] {'head'}, dimensions={0} | all-to-all | bytes 1048576 | tf_op jit(solution)/shard_map/all_to_all | solution.py:182
  (41 shorter events, 4.7 us)
Async XLA Ops:
  0.0 1.1 copy-start
  0.0 1.1 copy-start.1
  2.2 26.3 %copy-start.4 = (s32[1,6]{1,0:T(1,128)S(1)}, s32[1,6]{1,0:T(1,128)}, u32[]{:S(2)}) copy-start(s32[1,6]{1,0:T(1,128)} %param.12) | copy-start | bytes 76
  2.2 31.6 %copy-start.5 = (s32[64]{0:T(128)S(1)}, s32[64]{0:T(128)}, u32[]{:S(2)}) copy-start(s32[64]{0:T(128)} %param.13) | copy-start | bytes 772
  2.2 26.3 %all-to-all-start = ((bf16[8,64,768]{2,1,0:T(8,128)(2,1)}), bf16[8,64,768]{2,1,0:T(8,128)(2,1)S(1)}, u32[]{:S(2)}, u32[]{:S(2)}) async-start(bf16[8,64,768]{2,1,0:T(8,128)(2,1)} %pad_maximum_fusion), calls=%async_computation | async-start | bytes 1572864 | tf_op jit(solution)/shard_map/all_to_all | solution.py:118
  8.3 30.3 %copy-start.2 = (f32[4,6]{1,0:T(4,128)S(1)}, f32[4,6]{1,0:T(4,128)}, u32[]{:S(2)}) copy-start(f32[4,6]{1,0:T(4,128)} %param.10) | copy-start | bytes 292
  8.4 58.3 %collective-permute-start = (bf16[8,64,256]{2,1,0:T(8,128)(2,1)S(1)}, bf16[8,64,256]{2,1,0:T(8,128)(2,1)S(1)}, u32[]{:S(2)}, u32[]{:S(2)}) collective-permute-start(bf16[8,64,256]{2,1,0:T(8,128)(2,1)S(1)} %pad_maximum_fusion.2), channel_id=1, source_target_pairs={{0,128},{8,136},{16,144},{24,152},{32,160},{40,168},{48,176},{56,1... | collective-permute-start | bytes 786440 | tf_op jit(solution)/shard_map/ppermute | solution.py:16
  17.5 51.3 %collective-permute-start.1 = (bf16[8,64,256]{2,1,0:T(8,128)(2,1)S(1)}, bf16[8,64,256]{2,1,0:T(8,128)(2,1)}, u32[]{:S(2)}, u32[]{:S(2)}) collective-permute-start(bf16[8,64,256]{2,1,0:T(8,128)(2,1)S(1)} %pad_maximum_fusion.2), channel_id=1, source_target_pairs={{0,256},{8,264},{16,272},{24,280},{32,288},{40,296},{48,304},{56,3... | collective-permute-start | bytes 786440 | tf_op jit(solution)/shard_map/ppermute | solution.py:16
  28.5 20.5 %collective-permute-start.2 = (bf16[512,256]{1,0:T(8,128)(2,1)S(1)}, bf16[512,256]{1,0:T(8,128)(2,1)S(1)}, u32[]{:S(2)}, u32[]{:S(2)}) collective-permute-start(bf16[512,256]{1,0:T(8,128)(2,1)S(1)} %slice.14), channel_id=1, source_target_pairs={{0,8},{8,0},{16,24},{24,16},{32,40},{40,32},{48,56},{56,48},{64,72... | collective-permute-start | bytes 786440 | tf_op jit(solution)/shard_map/ppermute | solution.py:16
  30.5 25.4 %collective-permute-start.3 = (bf16[512,256]{1,0:T(8,128)(2,1)S(1)}, bf16[512,256]{1,0:T(8,128)(2,1)S(1)}, u32[]{:S(2)}, u32[]{:S(2)}) collective-permute-start(bf16[512,256]{1,0:T(8,128)(2,1)S(1)} %slice.14), channel_id=1, source_target_pairs={{0,16},{8,24},{16,0},{24,8},{32,48},{40,56},{48,32},{56,40},{64,80... | collective-permute-start | bytes 786440 | tf_op jit(solution)/shard_map/ppermute | solution.py:16
  34.6 7.8 %all-to-all-start.1 = ((bf16[4,64,256]{2,1,0:T(8,128)(2,1)}), bf16[4,64,256]{2,1,0:T(8,128)(2,1)S(1)}, u32[]{:S(2)}, u32[]{:S(2)}) async-start(bf16[4,64,256]{2,1,0:T(8,128)(2,1)} %broadcast_in_dim.5), calls=%async_computation.1 | async-start | bytes 262144 | tf_op jit(solution)/shard_map/all_to_all | solution.py:128
  43.1 32.2 %collective-permute-start.4 = (bf16[64,256]{1,0:T(8,128)(2,1)}, bf16[64,256]{1,0:T(8,128)(2,1)}, u32[]{:S(2)}, u32[]{:S(2)}) collective-permute-start(bf16[64,256]{1,0:T(8,128)(2,1)} %reduce_sum.22), channel_id=1, source_target_pairs={{0,384},{8,392},{16,400},{24,408},{32,416},{40,424},{48,432},{56,4... | collective-permute-start | bytes 98312 | tf_op jit(solution)/shard_map/ppermute | solution.py:16
  49.0 26.3 %collective-permute-start.5 = (bf16[64,256]{1,0:T(8,128)(2,1)}, bf16[64,256]{1,0:T(8,128)(2,1)}, u32[]{:S(2)}, u32[]{:S(2)}) collective-permute-start(bf16[64,256]{1,0:T(8,128)(2,1)} %reduce_sum.22), channel_id=1, source_target_pairs={{0,256},{8,264},{16,272},{24,280},{32,288},{40,296},{48,304},{56,3... | collective-permute-start | bytes 98312 | tf_op jit(solution)/shard_map/ppermute | solution.py:16
  55.9 19.5 %collective-permute-start.6 = (bf16[64,256]{1,0:T(8,128)(2,1)}, bf16[64,256]{1,0:T(8,128)(2,1)}, u32[]{:S(2)}, u32[]{:S(2)}) collective-permute-start(bf16[64,256]{1,0:T(8,128)(2,1)} %reduce_sum.22), channel_id=1, source_target_pairs={{0,128},{8,136},{16,144},{24,152},{32,160},{40,168},{48,176},{56,1... | collective-permute-start | bytes 98312 | tf_op jit(solution)/shard_map/ppermute | solution.py:16
  66.7 18.1 %collective-permute-start.7 = (bf16[512,256]{1,0:T(8,128)(2,1)S(1)}, bf16[512,256]{1,0:T(8,128)(2,1)S(1)}, u32[]{:S(2)}, u32[]{:S(2)}) collective-permute-start(bf16[512,256]{1,0:T(8,128)(2,1)S(1)} %slice.14), channel_id=1, source_target_pairs={{0,32},{8,40},{16,48},{24,56},{32,0},{40,8},{48,16},{56,24},{64,96... | collective-permute-start | bytes 786440 | tf_op jit(solution)/shard_map/ppermute | solution.py:16
  68.8 16.4 %collective-permute-start.8 = (bf16[512,256]{1,0:T(8,128)(2,1)S(1)}, bf16[512,256]{1,0:T(8,128)(2,1)S(1)}, u32[]{:S(2)}, u32[]{:S(2)}) collective-permute-start(bf16[512,256]{1,0:T(8,128)(2,1)S(1)} %slice.14), channel_id=1, source_target_pairs={{0,64},{8,72},{16,80},{24,88},{32,96},{40,104},{48,112},{56,120},{... | collective-permute-start | bytes 786440 | tf_op jit(solution)/shard_map/ppermute | solution.py:16
  75.3 19.3 %copy-start.3 = (f32[4]{0:T(128)S(1)}, f32[4]{0:T(128)}, u32[]{:S(2)}) copy-start(f32[4]{0:T(128)} %param.11) | copy-start | bytes 52
  77.1 20.7 %all-to-all-start.2 = ((bf16[8,64,512]{2,1,0:T(8,128)(2,1)}), bf16[8,64,512]{2,1,0:T(8,128)(2,1)S(1)}, u32[]{:S(2)}, u32[]{:S(2)}) async-start(bf16[8,64,512]{2,1,0:T(8,128)(2,1)} %pad_maximum_fusion.1), calls=%async_computation.2 | async-start | bytes 1048576 | tf_op jit(solution)/shard_map/all_to_all | solution.py:118
  85.2 9.5 %collective-permute-start.10 = (bf16[64,256]{1,0:T(8,128)(2,1)S(1)}, bf16[64,256]{1,0:T(8,128)(2,1)S(1)}, u32[]{:S(2)}, u32[]{:S(2)}) collective-permute-start(bf16[64,256]{1,0:T(8,128)(2,1)S(1)} %add_add_fusion.1), channel_id=1, source_target_pairs={{0,64},{8,72},{16,80},{24,88},{32,96},{40,104},{48,112},{56,120},{... | collective-permute-start | bytes 98312 | tf_op jit(solution)/shard_map/ppermute | solution.py:16
  87.1 7.6 %collective-permute-start.11 = (bf16[64,256]{1,0:T(8,128)(2,1)S(1)}, bf16[64,256]{1,0:T(8,128)(2,1)S(1)}, u32[]{:S(2)}, u32[]{:S(2)}) collective-permute-start(bf16[64,256]{1,0:T(8,128)(2,1)S(1)} %add_add_fusion.1), channel_id=1, source_target_pairs={{0,96},{8,104},{16,112},{24,120},{32,64},{40,72},{48,80},{56,88},{... | collective-permute-start | bytes 98312 | tf_op jit(solution)/shard_map/ppermute | solution.py:16
  92.0 5.8 %collective-permute-start.9 = (bf16[64,256]{1,0:T(8,128)(2,1)S(1)}, bf16[64,256]{1,0:T(8,128)(2,1)S(1)}, u32[]{:S(2)}, u32[]{:S(2)}) collective-permute-start(bf16[64,256]{1,0:T(8,128)(2,1)S(1)} %add_add_fusion.1), channel_id=1, source_target_pairs={{0,32},{8,40},{16,48},{24,56},{32,0},{40,8},{48,16},{56,24},{64,96... | collective-permute-start | bytes 98312 | tf_op jit(solution)/shard_map/ppermute | solution.py:16

commit v5 on v4

--- a/solution.py
+++ b/solution.py
@@ -163,7 +163,7 @@
     )
     far = to_heads(jnp.concatenate([shard4, shard5], axis=2))
     strided = plane + plane16 + plane32 + plane48
-    strided, level2, level3 = after((strided, level2, level3))
+    strided, level3 = after((strided, level3))
     anchors = strided + swap(strided, 4) + swap(strided, 8) + swap(strided, 12)
     count = anchors.shape[0]
     result = attend(

time: 123 us -> 122 us (level)
  the two profiles are of different devices: /device:TPU:8 before, /device:TPU:32 now
where the time goes in v5:
time: 122 us; the launch traced here: 121 us
  starting transfers between devices  76 us (62%)
  blocking collectives  16.8 us (14%)
  Pallas kernels  12.8 us (10%)
  waiting for transfers between devices  7.86 us (6%)
  local copies, waits for them, and re-layouts  3.47 us (3%)
  other arithmetic  3.39 us (3%)
    ppermute x12, starting transfers between devices, swap(): lax.ppermute(value, 'seq', [(i, i ^ bit) for i in range(lax.axis_size('se...  58.4 us
    all_to_all x1, blocking collectives, on_device(): lax.all_to_all(result, 'head', split_axis=0, concat_axis=1, tiled=True)  16.8 us
    all_to_all x2, starting transfers between devices, to_heads(): lax.all_to_all(array, 'head', split_axis=0, concat_axis=0, tiled=True)  14.3 us
    pallas_call x2, Pallas kernels, attend(): pl.pallas_call(functools.partial(attend_kernel, count, first, final), gri...  12.8 us
    all_to_all x1, waiting for transfers between devices, from_four(): lax.all_to_all(copies, 'seq', split_axis=0, concat_axis=0, axis_index_gro...  5.3 us
    all_to_all x1, starting transfers between devices, from_four(): lax.all_to_all(copies, 'seq', split_axis=0, concat_axis=0, axis_index_gro...  3.33 us
    ppermute x12, waiting for transfers between devices, swap(): lax.ppermute(value, 'seq', [(i, i ^ bit) for i in range(lax.axis_size('se...  2.55 us
  transfers between devices with their start and end apart: 15, of which 3 were waited for; matrix products, arithmetic and copies ran while one was open for 3% of the time, Pallas kernels for 5%

profile of v5, /device:TPU:32, one launch (start us, length us, event | category | flops | bytes accessed | tf_op | source)
XLA Modules:
  0.0 120.9 jit_solution(5898283117364216323)
XLA Ops:
  0.0 1.1 copy.23
  1.2 1.0 pad_maximum_fusion
  2.2 7.1 %all-to-all-start = ((bf16[8,64,768]{2,1,0:T(8,128)(2,1)}), bf16[8,64,768]{2,1,0:T(8,128)(2,1)S(1)}, u32[]{:S(2)}, u32[]{:S(2)}) async-start(bf16[8,64,768]{2,1,0:T(8,128)(2,1)} %pad_maximum_fusion), calls=%async_computation | async-start | bytes 1572864 | tf_op jit(solution)/shard_map/all_to_all | solution.py:118
  9.3 9.1 %collective-permute-start.1 = (bf16[8,64,256]{2,1,0:T(8,128)(2,1)S(1)}, bf16[8,64,256]{2,1,0:T(8,128)(2,1)S(1)}, u32[]{:S(2)}, u32[]{:S(2)}) collective-permute-start(bf16[8,64,256]{2,1,0:T(8,128)(2,1)S(1)} %pad_maximum_fusion.2), channel_id=1, source_target_pairs={{0,128},{8,136},{16,144},{24,152},{32,160},{40,168},{48,176},{56,1... | collective-permute-start | bytes 786440 | tf_op jit(solution)/shard_map/ppermute | solution.py:16
  18.4 10.0 %collective-permute-start.2 = (bf16[8,64,256]{2,1,0:T(8,128)(2,1)S(1)}, bf16[8,64,256]{2,1,0:T(8,128)(2,1)S(1)}, u32[]{:S(2)}, u32[]{:S(2)}) collective-permute-start(bf16[8,64,256]{2,1,0:T(8,128)(2,1)S(1)} %pad_maximum_fusion.2), channel_id=1, source_target_pairs={{0,256},{8,264},{16,272},{24,280},{32,288},{40,296},{48,304},{56,3... | collective-permute-start | bytes 786440 | tf_op jit(solution)/shard_map/ppermute | solution.py:16
  29.2 1.9 %collective-permute-start.3 = (bf16[512,256]{1,0:T(8,128)(2,1)}, bf16[512,256]{1,0:T(8,128)(2,1)S(1)}, u32[]{:S(2)}, u32[]{:S(2)}) collective-permute-start(bf16[512,256]{1,0:T(8,128)(2,1)} %slice.14), channel_id=1, source_target_pairs={{0,8},{8,0},{16,24},{24,16},{32,40},{40,32},{48,56},{56,48},{64,72... | collective-permute-start | bytes 786440 | tf_op jit(solution)/shard_map/ppermute | solution.py:16
  31.2 2.6 %collective-permute-start.4 = (bf16[512,256]{1,0:T(8,128)(2,1)}, bf16[512,256]{1,0:T(8,128)(2,1)S(1)}, u32[]{:S(2)}, u32[]{:S(2)}) collective-permute-start(bf16[512,256]{1,0:T(8,128)(2,1)} %slice.14), channel_id=1, source_target_pairs={{0,16},{8,24},{16,0},{24,8},{32,48},{40,56},{48,32},{56,40},{64,80... | collective-permute-start | bytes 786440 | tf_op jit(solution)/shard_map/ppermute | solution.py:16
  34.6 3.3 %all-to-all-start.1 = ((bf16[4,64,256]{2,1,0:T(8,128)(2,1)}), bf16[4,64,256]{2,1,0:T(8,128)(2,1)S(1)}, u32[]{:S(2)}, u32[]{:S(2)}) async-start(bf16[4,64,256]{2,1,0:T(8,128)(2,1)} %broadcast_in_dim.5), calls=%async_computation.1 | async-start | bytes 262144 | tf_op jit(solution)/shard_map/all_to_all | solution.py:128
  38.1 5.3 %all-to-all-done.1 = bf16[4,64,256]{2,1,0:T(8,128)(2,1)S(1)} async-done(((bf16[4,64,256]{2,1,0:T(8,128)(2,1)}), bf16[4,64,256]{2,1,0:T(8,128)(2,1)S(1)}, u32[]{:S(2)}, u32[]{:S(2)}) %all-to-all-start.1) | async-done | bytes 131104 | tf_op jit(solution)/shard_map/all_to_all | solution.py:128
  44.0 5.9 %collective-permute-start.5 = (bf16[64,256]{1,0:T(8,128)(2,1)}, bf16[64,256]{1,0:T(8,128)(2,1)}, u32[]{:S(2)}, u32[]{:S(2)}) collective-permute-start(bf16[64,256]{1,0:T(8,128)(2,1)} %reduce_sum.22), channel_id=1, source_target_pairs={{0,384},{8,392},{16,400},{24,408},{32,416},{40,424},{48,432},{56,4... | collective-permute-start | bytes 98312 | tf_op jit(solution)/shard_map/ppermute | solution.py:16
  49.9 6.8 %collective-permute-start.6 = (bf16[64,256]{1,0:T(8,128)(2,1)}, bf16[64,256]{1,0:T(8,128)(2,1)}, u32[]{:S(2)}, u32[]{:S(2)}) collective-permute-start(bf16[64,256]{1,0:T(8,128)(2,1)} %reduce_sum.22), channel_id=1, source_target_pairs={{0,256},{8,264},{16,272},{24,280},{32,288},{40,296},{48,304},{56,3... | collective-permute-start | bytes 98312 | tf_op jit(solution)/shard_map/ppermute | solution.py:16
  56.8 4.3 %collective-permute-start.7 = (bf16[64,256]{1,0:T(8,128)(2,1)}, bf16[64,256]{1,0:T(8,128)(2,1)}, u32[]{:S(2)}, u32[]{:S(2)}) collective-permute-start(bf16[64,256]{1,0:T(8,128)(2,1)} %reduce_sum.22), channel_id=1, source_target_pairs={{0,128},{8,136},{16,144},{24,152},{32,160},{40,168},{48,176},{56,1... | collective-permute-start | bytes 98312 | tf_op jit(solution)/shard_map/ppermute | solution.py:16
  61.1 5.6 %shard_map.73 = (f32[512,512]{1,0:T(8,128)S(1)}, f32[512,8]{1,0:T(8,128)S(1)}) custom-call(f32[3,4]{1,0:T(4,128)S(1)} %pad_slice_fusion.bias_ref, bf16[512,768]{1,0:T(8,128)(2,1)S(1)} %bitcast.30, bf16[512,768]{1,0:T(8,128)(2,1)S(1)} %bitcast.31, bf16[512,768]{1,0:T(8,128)(2,1)S(1)} %bitcast.32, bf16[512,256]{1,0:T(8,128)(2,1)S(1)} %collective-permute-done.3.refs_2_.refs_3_, ...), custom_call_target="tpu_custom_call" | custom-call | tf_op jit(solution)/shard_map/pallas_call | solution.py:93
  66.7 3.4 %collective-permute-start.8 = (bf16[512,256]{1,0:T(8,128)(2,1)}, bf16[512,256]{1,0:T(8,128)(2,1)S(1)}, u32[]{:S(2)}, u32[]{:S(2)}) collective-permute-start(bf16[512,256]{1,0:T(8,128)(2,1)} %slice.14), channel_id=1, source_target_pairs={{0,64},{8,72},{16,80},{24,88},{32,96},{40,104},{48,112},{56,120},{... | collective-permute-start | bytes 786440 | tf_op jit(solution)/shard_map/ppermute | solution.py:16
  70.1 2.9 %collective-permute-start = (bf16[512,256]{1,0:T(8,128)(2,1)}, bf16[512,256]{1,0:T(8,128)(2,1)S(1)}, u32[]{:S(2)}, u32[]{:S(2)}) collective-permute-start(bf16[512,256]{1,0:T(8,128)(2,1)} %slice.14), channel_id=1, source_target_pairs={{0,32},{8,40},{16,48},{24,56},{32,0},{40,8},{48,16},{56,24},{64,96... | collective-permute-start | bytes 786440 | tf_op jit(solution)/shard_map/ppermute | solution.py:16
  73.1 0.8 pad_maximum_fusion.1
  73.9 7.2 %all-to-all-start.2 = ((bf16[8,64,512]{2,1,0:T(8,128)(2,1)}), bf16[8,64,512]{2,1,0:T(8,128)(2,1)S(1)}, u32[]{:S(2)}, u32[]{:S(2)}) async-start(bf16[8,64,512]{2,1,0:T(8,128)(2,1)} %pad_maximum_fusion.1), calls=%async_computation.2 | async-start | bytes 1048576 | tf_op jit(solution)/shard_map/all_to_all | solution.py:118
  81.9 6.0 %collective-permute-start.10 = (bf16[64,256]{1,0:T(8,128)(2,1)S(1)}, bf16[64,256]{1,0:T(8,128)(2,1)S(1)}, u32[]{:S(2)}, u32[]{:S(2)}) collective-permute-start(bf16[64,256]{1,0:T(8,128)(2,1)S(1)} %add_add_fusion.1), channel_id=1, source_target_pairs={{0,64},{8,72},{16,80},{24,88},{32,96},{40,104},{48,112},{56,120},{... | collective-permute-start | bytes 98312 | tf_op jit(solution)/shard_map/ppermute | solution.py:16
  88.0 2.2 %collective-permute-start.11 = (bf16[64,256]{1,0:T(8,128)(2,1)S(1)}, bf16[64,256]{1,0:T(8,128)(2,1)S(1)}, u32[]{:S(2)}, u32[]{:S(2)}) collective-permute-start(bf16[64,256]{1,0:T(8,128)(2,1)S(1)} %add_add_fusion.1), channel_id=1, source_target_pairs={{0,96},{8,104},{16,112},{24,120},{32,64},{40,72},{48,80},{56,88},{... | collective-permute-start | bytes 98312 | tf_op jit(solution)/shard_map/ppermute | solution.py:16
  90.2 3.2 %collective-permute-start.9 = (bf16[64,256]{1,0:T(8,128)(2,1)S(1)}, bf16[64,256]{1,0:T(8,128)(2,1)S(1)}, u32[]{:S(2)}, u32[]{:S(2)}) collective-permute-start(bf16[64,256]{1,0:T(8,128)(2,1)S(1)} %add_add_fusion.1), channel_id=1, source_target_pairs={{0,32},{8,40},{16,48},{24,56},{32,0},{40,8},{48,16},{56,24},{64,96... | collective-permute-start | bytes 98312 | tf_op jit(solution)/shard_map/ppermute | solution.py:16
  93.8 2.3 %collective-permute-done.9 = bf16[64,256]{1,0:T(8,128)(2,1)S(1)} collective-permute-done((bf16[64,256]{1,0:T(8,128)(2,1)S(1)}, bf16[64,256]{1,0:T(8,128)(2,1)S(1)}, u32[]{:S(2)}, u32[]{:S(2)}) %collective-permute-start.9) | collective-permute-done | bytes 32800 | tf_op jit(solution)/shard_map/ppermute | solution.py:16
  96.1 7.1 %shard_map.74 = bf16[512,512]{1,0:T(8,128)(2,1)S(1)} custom-call(f32[5,4]{1,0:T(8,128)S(1)} %slice.11.bias_ref, bf16[512,768]{1,0:T(8,128)(2,1)S(1)} %bitcast.33, bf16[512,256]{1,0:T(8,128)(2,1)S(1)} %collective-permute-done.refs_0_.refs_1_, bf16[512,256]{1,0:T(8,128)(2,1)S(1)} %collective-permute-done.refs_0_.refs_1_, ...), custom_call_target="tpu_custom_call" | custom-call | tf_op jit(solution)/shard_map/pallas_call | solution.py:93
  103.2 16.8 %all_to_all.34 = bf16[8,64,512]{2,1,0:T(8,128)(2,1)S(1)} all-to-all(bf16[8,64,512]{2,1,0:T(8,128)(2,1)S(1)} %bitcast.38), channel_id=1, replica_groups=mesh['seq'=64,'head'=8] {'head'}, dimensions={0} | all-to-all | bytes 1048576 | tf_op jit(solution)/shard_map/all_to_all | solution.py:182
  120.1 0.8 copy.19
  (41 shorter events, 3.6 us)
Async XLA Ops:
  0.0 1.1 copy-start
  0.0 1.1 copy-start.1
  2.2 26.3 %copy-start.4 = (s32[1,6]{1,0:T(1,128)S(1)}, s32[1,6]{1,0:T(1,128)}, u32[]{:S(2)}) copy-start(s32[1,6]{1,0:T(1,128)} %param.12) | copy-start | bytes 76
  2.2 31.6 %copy-start.5 = (s32[64]{0:T(128)S(1)}, s32[64]{0:T(128)}, u32[]{:S(2)}) copy-start(s32[64]{0:T(128)} %param.13) | copy-start | bytes 772
  2.2 26.3 %all-to-all-start = ((bf16[8,64,768]{2,1,0:T(8,128)(2,1)}), bf16[8,64,768]{2,1,0:T(8,128)(2,1)S(1)}, u32[]{:S(2)}, u32[]{:S(2)}) async-start(bf16[8,64,768]{2,1,0:T(8,128)(2,1)} %pad_maximum_fusion), calls=%async_computation | async-start | bytes 1572864 | tf_op jit(solution)/shard_map/all_to_all | solution.py:118
  9.2 28.7 %copy-start.2 = (f32[4,6]{1,0:T(4,128)S(1)}, f32[4,6]{1,0:T(4,128)}, u32[]{:S(2)}) copy-start(f32[4,6]{1,0:T(4,128)} %param.10) | copy-start | bytes 292
  9.3 57.4 %collective-permute-start.1 = (bf16[8,64,256]{2,1,0:T(8,128)(2,1)S(1)}, bf16[8,64,256]{2,1,0:T(8,128)(2,1)S(1)}, u32[]{:S(2)}, u32[]{:S(2)}) collective-permute-start(bf16[8,64,256]{2,1,0:T(8,128)(2,1)S(1)} %pad_maximum_fusion.2), channel_id=1, source_target_pairs={{0,128},{8,136},{16,144},{24,152},{32,160},{40,168},{48,176},{56,1... | collective-permute-start | bytes 786440 | tf_op jit(solution)/shard_map/ppermute | solution.py:16
  18.4 51.7 %collective-permute-start.2 = (bf16[8,64,256]{2,1,0:T(8,128)(2,1)S(1)}, bf16[8,64,256]{2,1,0:T(8,128)(2,1)S(1)}, u32[]{:S(2)}, u32[]{:S(2)}) collective-permute-start(bf16[8,64,256]{2,1,0:T(8,128)(2,1)S(1)} %pad_maximum_fusion.2), channel_id=1, source_target_pairs={{0,256},{8,264},{16,272},{24,280},{32,288},{40,296},{48,304},{56,3... | collective-permute-start | bytes 786440 | tf_op jit(solution)/shard_map/ppermute | solution.py:16
  29.2 20.7 %collective-permute-start.3 = (bf16[512,256]{1,0:T(8,128)(2,1)}, bf16[512,256]{1,0:T(8,128)(2,1)S(1)}, u32[]{:S(2)}, u32[]{:S(2)}) collective-permute-start(bf16[512,256]{1,0:T(8,128)(2,1)} %slice.14), channel_id=1, source_target_pairs={{0,8},{8,0},{16,24},{24,16},{32,40},{40,32},{48,56},{56,48},{64,72... | collective-permute-start | bytes 786440 | tf_op jit(solution)/shard_map/ppermute | solution.py:16
  31.2 25.6 %collective-permute-start.4 = (bf16[512,256]{1,0:T(8,128)(2,1)}, bf16[512,256]{1,0:T(8,128)(2,1)S(1)}, u32[]{:S(2)}, u32[]{:S(2)}) collective-permute-start(bf16[512,256]{1,0:T(8,128)(2,1)} %slice.14), channel_id=1, source_target_pairs={{0,16},{8,24},{16,0},{24,8},{32,48},{40,56},{48,32},{56,40},{64,80... | collective-permute-start | bytes 786440 | tf_op jit(solution)/shard_map/ppermute | solution.py:16
  34.6 8.7 %all-to-all-start.1 = ((bf16[4,64,256]{2,1,0:T(8,128)(2,1)}), bf16[4,64,256]{2,1,0:T(8,128)(2,1)S(1)}, u32[]{:S(2)}, u32[]{:S(2)}) async-start(bf16[4,64,256]{2,1,0:T(8,128)(2,1)} %broadcast_in_dim.5), calls=%async_computation.1 | async-start | bytes 262144 | tf_op jit(solution)/shard_map/all_to_all | solution.py:128
  44.0 29.0 %collective-permute-start.5 = (bf16[64,256]{1,0:T(8,128)(2,1)}, bf16[64,256]{1,0:T(8,128)(2,1)}, u32[]{:S(2)}, u32[]{:S(2)}) collective-permute-start(bf16[64,256]{1,0:T(8,128)(2,1)} %reduce_sum.22), channel_id=1, source_target_pairs={{0,384},{8,392},{16,400},{24,408},{32,416},{40,424},{48,432},{56,4... | collective-permute-start | bytes 98312 | tf_op jit(solution)/shard_map/ppermute | solution.py:16
  49.9 23.2 %collective-permute-start.6 = (bf16[64,256]{1,0:T(8,128)(2,1)}, bf16[64,256]{1,0:T(8,128)(2,1)}, u32[]{:S(2)}, u32[]{:S(2)}) collective-permute-start(bf16[64,256]{1,0:T(8,128)(2,1)} %reduce_sum.22), channel_id=1, source_target_pairs={{0,256},{8,264},{16,272},{24,280},{32,288},{40,296},{48,304},{56,3... | collective-permute-start | bytes 98312 | tf_op jit(solution)/shard_map/ppermute | solution.py:16
  56.8 16.3 %collective-permute-start.7 = (bf16[64,256]{1,0:T(8,128)(2,1)}, bf16[64,256]{1,0:T(8,128)(2,1)}, u32[]{:S(2)}, u32[]{:S(2)}) collective-permute-start(bf16[64,256]{1,0:T(8,128)(2,1)} %reduce_sum.22), channel_id=1, source_target_pairs={{0,128},{8,136},{16,144},{24,152},{32,160},{40,168},{48,176},{56,1... | collective-permute-start | bytes 98312 | tf_op jit(solution)/shard_map/ppermute | solution.py:16
  66.7 15.2 %collective-permute-start.8 = (bf16[512,256]{1,0:T(8,128)(2,1)}, bf16[512,256]{1,0:T(8,128)(2,1)S(1)}, u32[]{:S(2)}, u32[]{:S(2)}) collective-permute-start(bf16[512,256]{1,0:T(8,128)(2,1)} %slice.14), channel_id=1, source_target_pairs={{0,64},{8,72},{16,80},{24,88},{32,96},{40,104},{48,112},{56,120},{... | collective-permute-start | bytes 786440 | tf_op jit(solution)/shard_map/ppermute | solution.py:16
  70.1 25.9 %collective-permute-start = (bf16[512,256]{1,0:T(8,128)(2,1)}, bf16[512,256]{1,0:T(8,128)(2,1)S(1)}, u32[]{:S(2)}, u32[]{:S(2)}) collective-permute-start(bf16[512,256]{1,0:T(8,128)(2,1)} %slice.14), channel_id=1, source_target_pairs={{0,32},{8,40},{16,48},{24,56},{32,0},{40,8},{48,16},{56,24},{64,96... | collective-permute-start | bytes 786440 | tf_op jit(solution)/shard_map/ppermute | solution.py:16
  73.1 20.4 %copy-start.3 = (f32[4]{0:T(128)S(1)}, f32[4]{0:T(128)}, u32[]{:S(2)}) copy-start(f32[4]{0:T(128)} %param.11) | copy-start | bytes 52
  73.9 22.1 %all-to-all-start.2 = ((bf16[8,64,512]{2,1,0:T(8,128)(2,1)}), bf16[8,64,512]{2,1,0:T(8,128)(2,1)S(1)}, u32[]{:S(2)}, u32[]{:S(2)}) async-start(bf16[8,64,512]{2,1,0:T(8,128)(2,1)} %pad_maximum_fusion.1), calls=%async_computation.2 | async-start | bytes 1048576 | tf_op jit(solution)/shard_map/all_to_all | solution.py:118
  81.9 11.5 %collective-permute-start.10 = (bf16[64,256]{1,0:T(8,128)(2,1)S(1)}, bf16[64,256]{1,0:T(8,128)(2,1)S(1)}, u32[]{:S(2)}, u32[]{:S(2)}) collective-permute-start(bf16[64,256]{1,0:T(8,128)(2,1)S(1)} %add_add_fusion.1), channel_id=1, source_target_pairs={{0,64},{8,72},{16,80},{24,88},{32,96},{40,104},{48,112},{56,120},{... | collective-permute-start | bytes 98312 | tf_op jit(solution)/shard_map/ppermute | solution.py:16
  88.0 5.8 %collective-permute-start.11 = (bf16[64,256]{1,0:T(8,128)(2,1)S(1)}, bf16[64,256]{1,0:T(8,128)(2,1)S(1)}, u32[]{:S(2)}, u32[]{:S(2)}) collective-permute-start(bf16[64,256]{1,0:T(8,128)(2,1)S(1)} %add_add_fusion.1), channel_id=1, source_target_pairs={{0,96},{8,104},{16,112},{24,120},{32,64},{40,72},{48,80},{56,88},{... | collective-permute-start | bytes 98312 | tf_op jit(solution)/shard_map/ppermute | solution.py:16
  90.2 5.8 %collective-permute-start.9 = (bf16[64,256]{1,0:T(8,128)(2,1)S(1)}, bf16[64,256]{1,0:T(8,128)(2,1)S(1)}, u32[]{:S(2)}, u32[]{:S(2)}) collective-permute-start(bf16[64,256]{1,0:T(8,128)(2,1)S(1)} %add_add_fusion.1), channel_id=1, source_target_pairs={{0,32},{8,40},{16,48},{24,56},{32,0},{40,8},{48,16},{56,24},{64,96... | collective-permute-start | bytes 98312 | tf_op jit(solution)/shard_map/ppermute | solution.py:16
